TPU v7x, 32 devices: a whole 2x2x4 slice. The times are simulated.
32 devices in a mesh: fsdp: 8 (over y, x, core), ctx: 4 (over z).
Axes of the slice: x: 2, y: 2, z: 4, core: 2. Of those that a mesh axis runs over, the one named last changes fastest.
Arguments:
- tokens: bfloat16 [8, 2048, 1024], P('fsdp', 'ctx'), may hold values from -6 to 6
- query_key_value_weight: bfloat16 [1024, 3072], P('fsdp'), may hold values from -0.1875 to 0.1875
- attention_output_weight: bfloat16 [1024, 1024], P('fsdp'), may hold values from -6 to 6
- geglu_input_weight: bfloat16 [1024, 5248], P('fsdp'), may hold values from -0.1875 to 0.1875
- geglu_output_weight: bfloat16 [2624, 1024], P(None, 'fsdp'), may hold values from -0.125 to 0.125
- gain_one: bfloat16 [1024], P('fsdp'), may hold values from 0.5 to 1.5
- gain_two: bfloat16 [1024], P('fsdp'), may hold values from 0.5 to 1.5
- cotangent: bfloat16 [8, 2048, 1024], P('fsdp', 'ctx'), may hold values from -6 to 6
Outputs:
- mixed: bfloat16 [8, 2048, 1024], P('fsdp', 'ctx')
- grad_tokens: float32 [8, 2048, 1024], P('fsdp', 'ctx')
- grad_qkv: float32 [1024, 3072], P('fsdp')
- grad_attn_out: float32 [1024, 1024], P('fsdp')
- grad_in: float32 [1024, 5248], P('fsdp')
- grad_out: float32 [2624, 1024], P(None, 'fsdp')
- grad_gain_one: float32 [1024], P('fsdp')
- grad_gain_two: float32 [1024], P('fsdp')
All inputs are finite; a program needn't handle non-finite values.
Results may differ from a plain program's by a relative error of at most 0.023.
Values may be sent and summed in bfloat16 or wider, within the bound.
A program may use at most 384 MiB of HBM per device.

v0:
```python
import math

import jax
import jax.numpy as jnp
from jax import lax
from jax.sharding import PartitionSpec as P

HEADS = 16
HEAD_DIM = 64


EPSILON = 1e-05
ROPE_BASE = 160000.0


def normalize(values):
    row_mean = jnp.mean(values, -1, keepdims=True)
    centered = values - row_mean
    variance = jnp.mean(centered * centered, -1, keepdims=True)
    inv_std = lax.rsqrt(variance + EPSILON)
    return (centered * inv_std, inv_std)


def norm_back(grad_normed, normed, inv_std):
    first_mean = jnp.mean(grad_normed, -1, keepdims=True)
    second_mean = jnp.mean(grad_normed * normed, -1, keepdims=True)
    return inv_std * (grad_normed - first_mean - normed * second_mean)


def rope_tables(first_row, local_rows):
    positions = (first_row + jnp.arange(local_rows, dtype=jnp.int32)).astype(jnp.float32)
    inv_freq = ROPE_BASE ** (-(jnp.arange(HEAD_DIM // 2, dtype=jnp.float32) * 2.0 / HEAD_DIM))
    angles = positions[:, None] * inv_freq[None, :]
    angles = jnp.concatenate([angles, angles], -1)
    return (jnp.cos(angles)[:, None, :], jnp.sin(angles)[:, None, :])


def rotate(vectors, cosine, sine):
    half_dim = vectors.shape[-1] // 2
    turned = jnp.concatenate([-vectors[..., half_dim:], vectors[..., :half_dim]], -1)
    return vectors * cosine + turned * sine


def local(
    tokens,
    query_key_value_weight,
    attention_output_weight,
    geglu_input_weight,
    geglu_output_weight,
    gain_one,
    gain_two,
    cotangent,
):
    local_rows = tokens.shape[1]
    model_width = tokens.shape[2]
    hidden_width = geglu_output_weight.shape[0]
    score_scale = HEAD_DIM ** (-0.5)
    full_qkv, full_attn, full_in, full_out, full_one, full_two = (
        lax.all_gather(query_key_value_weight, "fsdp", axis=0, tiled=True),
        lax.all_gather(attention_output_weight, "fsdp", axis=0, tiled=True),
        lax.all_gather(geglu_input_weight, "fsdp", axis=0, tiled=True),
        lax.all_gather(geglu_output_weight, "fsdp", axis=1, tiled=True),
        lax.all_gather(gain_one, "fsdp", axis=0, tiled=True),
        lax.all_gather(gain_two, "fsdp", axis=0, tiled=True),
    )
    inputs = tokens[0].astype(jnp.float32)
    normed_one, inv_one = normalize(inputs)
    hidden_after_attention = (normed_one * full_one.astype(jnp.float32)).astype(jnp.bfloat16)
    query_key_value = jnp.dot(hidden_after_attention, full_qkv, preferred_element_type=jnp.float32)
    cosine, sine = rope_tables(lax.axis_index("ctx") * local_rows, local_rows)
    head_shape = (local_rows, HEADS, HEAD_DIM)
    query = rotate(query_key_value[:, :model_width].reshape(head_shape), cosine, sine).astype(
        jnp.bfloat16
    )
    keys = rotate(
        query_key_value[:, model_width : 2 * model_width].reshape(head_shape), cosine, sine
    ).astype(jnp.bfloat16)
    keys = keys.reshape(local_rows, model_width)
    values = query_key_value[:, 2 * model_width :].astype(jnp.bfloat16)
    running_max = jnp.full((HEADS, local_rows), -1e30, jnp.float32)
    key_block = lax.all_gather(keys, "ctx", axis=0, tiled=True)
    value_block = lax.all_gather(values, "ctx", axis=0, tiled=True)
    count = key_block.shape[0]
    key_heads = key_block.reshape(count, HEADS, HEAD_DIM)
    value_heads = value_block.reshape(count, HEADS, HEAD_DIM)
    scores = (
        jnp.einsum("qhd,khd->hqk", query, key_heads, preferred_element_type=jnp.float32)
        * score_scale
    )
    new_max = jnp.maximum(running_max, jnp.max(scores, -1))
    weights = jnp.exp(scores - new_max[..., None])
    running_sum = jnp.sum(weights, -1)
    summed = jnp.einsum(
        "hqk,khd->hqd",
        weights.astype(jnp.bfloat16),
        value_heads,
        preferred_element_type=jnp.float32,
    )
    summed, running_max, running_sum = (summed, new_max, running_sum)
    attn_heads = summed / running_sum[..., None]
    log_total = running_max + jnp.log(running_sum)
    attn_rows = jnp.transpose(attn_heads, (1, 0, 2))
    attn_low = attn_rows.reshape(local_rows, model_width).astype(jnp.bfloat16)
    middle_activation = inputs + jnp.dot(attn_low, full_attn, preferred_element_type=jnp.float32)
    normed_two, inv_two = normalize(middle_activation)
    hidden_after_feedforward = (normed_two * full_two.astype(jnp.float32)).astype(jnp.bfloat16)
    projected_up_rows = jnp.dot(
        hidden_after_feedforward, full_in, preferred_element_type=jnp.float32
    )
    gate_in = projected_up_rows[:, :hidden_width]
    gate_up = projected_up_rows[:, hidden_width:]
    normal_cdf = 0.5 * (1.0 + lax.erf(gate_in * (1.0 / math.sqrt(2.0))))
    normal_pdf = jnp.exp(-0.5 * gate_in * gate_in) * (1.0 / math.sqrt(2.0 * math.pi))
    activated = gate_in * normal_cdf
    hidden_state = (activated * gate_up).astype(jnp.bfloat16)
    mixed = (
        middle_activation + jnp.dot(hidden_state, full_out, preferred_element_type=jnp.float32)
    ).astype(jnp.bfloat16)
    back_qkv, back_attn, back_in, back_out, back_one, back_two = (
        full_qkv,
        full_attn,
        full_in,
        full_out,
        full_one,
        full_two,
    )
    grad_mixed = cotangent[0]
    grad_wout = jnp.einsum(
        "rf,rd->fd", hidden_state, grad_mixed, preferred_element_type=jnp.float32
    )
    grad_hidden = jnp.einsum("rd,fd->rf", grad_mixed, back_out, preferred_element_type=jnp.float32)
    grad_up = jnp.concatenate(
        [grad_hidden * gate_up * (normal_cdf + gate_in * normal_pdf), grad_hidden * activated], -1
    ).astype(jnp.bfloat16)
    grad_win = jnp.einsum(
        "rd,rf->df", hidden_after_feedforward, grad_up, preferred_element_type=jnp.float32
    )
    grad_htwo = jnp.einsum("rf,df->rd", grad_up, back_in, preferred_element_type=jnp.float32)
    grad_two = jnp.sum(grad_htwo * normed_two, 0)
    grad_middle = grad_mixed.astype(jnp.float32) + norm_back(
        grad_htwo * back_two.astype(jnp.float32), normed_two, inv_two
    )
    ffn_parts = (
        lax.psum_scatter(
            grad_win.astype(jnp.bfloat16), "fsdp", scatter_dimension=0, tiled=True
        ).astype(jnp.float32),
        lax.psum_scatter(
            grad_wout.astype(jnp.bfloat16), "fsdp", scatter_dimension=1, tiled=True
        ).astype(jnp.float32),
        lax.psum_scatter(
            grad_two.astype(jnp.bfloat16), "fsdp", scatter_dimension=0, tiled=True
        ).astype(jnp.float32),
    )
    sum_win, sum_wout, sum_two = (
        lax.psum(ffn_parts[0].astype(jnp.bfloat16), "ctx").astype(jnp.float32),
        lax.psum(ffn_parts[1].astype(jnp.bfloat16), "ctx").astype(jnp.float32),
        lax.psum(ffn_parts[2].astype(jnp.bfloat16), "ctx").astype(jnp.float32),
    )
    grad_branch = grad_middle.astype(jnp.bfloat16)
    grad_wattn = jnp.einsum("rd,re->de", attn_low, grad_branch, preferred_element_type=jnp.float32)
    grad_attn = jnp.einsum("re,de->rd", grad_branch, back_attn, preferred_element_type=jnp.float32)
    grad_attn = grad_attn.astype(jnp.bfloat16).reshape(head_shape)
    delta = jnp.einsum("qhd,qhd->hq", grad_attn.astype(jnp.float32), attn_rows)

    def block_terms(key_heads, value_heads):
        scores = (
            jnp.einsum("qhd,khd->hqk", query, key_heads, preferred_element_type=jnp.float32)
            * score_scale
        )
        probs = jnp.exp(scores - log_total[..., None])
        grad_probs = jnp.einsum(
            "qhd,khd->hqk", grad_attn, value_heads, preferred_element_type=jnp.float32
        )
        grad_scores = (probs * (grad_probs - delta[..., None])).astype(jnp.bfloat16)
        return (probs, grad_scores)

    key_block = lax.all_gather(keys, "ctx", axis=0, tiled=True)
    value_block = lax.all_gather(values, "ctx", axis=0, tiled=True)
    count = key_block.shape[0]
    key_heads = key_block.reshape(count, HEADS, HEAD_DIM)
    value_heads = value_block.reshape(count, HEADS, HEAD_DIM)
    probs, grad_scores = block_terms(key_heads, value_heads)
    grad_query = (
        jnp.einsum("hqk,khd->qhd", grad_scores, key_heads, preferred_element_type=jnp.float32)
        * score_scale
    )
    key_value_rows = jnp.concatenate([keys, values], -1)
    piece = lax.all_gather(key_value_rows, "ctx", axis=0, tiled=True)
    count = piece.shape[0]
    key_heads = piece[:, :model_width].reshape(count, HEADS, HEAD_DIM)
    value_heads = piece[:, model_width:].reshape(count, HEADS, HEAD_DIM)
    probs, grad_scores = block_terms(key_heads, value_heads)
    grad_keys = (
        jnp.einsum("hqk,qhd->khd", grad_scores, query, preferred_element_type=jnp.float32)
        * score_scale
    )
    grad_values = jnp.einsum(
        "hqk,qhd->khd", probs.astype(jnp.bfloat16), grad_attn, preferred_element_type=jnp.float32
    )
    grad_kv = jnp.concatenate(
        [grad_keys.reshape(count, model_width), grad_values.reshape(count, model_width)], -1
    )
    own_kv = lax.psum_scatter(
        grad_kv.astype(jnp.bfloat16), "ctx", scatter_dimension=0, tiled=True
    ).astype(jnp.float32)
    grad_q = rotate(grad_query, cosine, -sine).reshape(local_rows, model_width)
    grad_k = rotate(own_kv[:, :model_width].reshape(head_shape), cosine, -sine).reshape(
        local_rows, model_width
    )
    grad_qkv_rows = jnp.concatenate([grad_q, grad_k, own_kv[:, model_width:]], -1).astype(
        jnp.bfloat16
    )
    grad_wqkv = jnp.einsum(
        "rd,re->de", hidden_after_attention, grad_qkv_rows, preferred_element_type=jnp.float32
    )
    grad_hone = jnp.einsum("re,de->rd", grad_qkv_rows, back_qkv, preferred_element_type=jnp.float32)
    grad_one = jnp.sum(grad_hone * normed_one, 0)
    grad_inputs = grad_middle + norm_back(
        grad_hone * back_one.astype(jnp.float32), normed_one, inv_one
    )
    attn_parts = (
        lax.psum_scatter(
            grad_wqkv.astype(jnp.bfloat16), "fsdp", scatter_dimension=0, tiled=True
        ).astype(jnp.float32),
        lax.psum_scatter(
            grad_wattn.astype(jnp.bfloat16), "fsdp", scatter_dimension=0, tiled=True
        ).astype(jnp.float32),
        lax.psum_scatter(
            grad_one.astype(jnp.bfloat16), "fsdp", scatter_dimension=0, tiled=True
        ).astype(jnp.float32),
    )
    sum_wqkv, sum_wattn, sum_one = (
        lax.psum(attn_parts[0].astype(jnp.bfloat16), "ctx").astype(jnp.float32),
        lax.psum(attn_parts[1].astype(jnp.bfloat16), "ctx").astype(jnp.float32),
        lax.psum(attn_parts[2].astype(jnp.bfloat16), "ctx").astype(jnp.float32),
    )
    return (
        mixed[None],
        grad_inputs[None],
        sum_wqkv,
        sum_wattn,
        sum_win,
        sum_wout,
        sum_one,
        sum_two,
    )


def solution(mesh):
    placed = (
        P("fsdp", "ctx", None),
        P("fsdp", None),
        P("fsdp", None),
        P("fsdp", None),
        P(None, "fsdp"),
        P("fsdp"),
        P("fsdp"),
        P("fsdp", "ctx", None),
    )
    return jax.shard_map(
        local,
        mesh=mesh,
        in_specs=placed,
        out_specs=(
            P("fsdp", "ctx", None),
            P("fsdp", "ctx", None),
            P("fsdp", None),
            P("fsdp", None),
            P("fsdp", None),
            P(None, "fsdp"),
            P("fsdp"),
            P("fsdp"),
        ),
        check_vma=False,
    )
```

profile of v0, /device:TPU:0, one launch (start us, length us, event | category | flops | bytes accessed | tf_op | source)
XLA Modules:
  0.0 1174.2 jit_solution(17614798387492227086)
XLA Ops:
  8.0 10.3 all-gather
  22.1 36.1 %all-gather.10.cloned.1.call-done = bf16[1024,3072]{1,0:T(8,128)(2,1)} async-done(((bf16[128,3072]{1,0:T(8,128)(2,1)}), bf16[1024,3072]{1,0:T(8,128)(2,1)}) %all-gather.10.cloned.1.call-update) | async-done | bytes 6291472 | tf_op jit(solution)/shard_map/all_gather | solution.py:59
  58.1 5.7 fusion.68
  63.9 2.6 copy-done.6
  72.2 5.9 add_convert_fusion.1
  78.2 2.7 slice.118
  82.8 8.7 all-gather.1
  93.4 3.1 pad_maximum_fusion.5
  98.6 60.5 %all-gather.12.cloned.1.call-done = bf16[2048,1024]{1,0:T(8,128)(2,1)} async-done(((bf16[512,1024]{1,0:T(8,128)(2,1)}), bf16[2048,1024]{1,0:T(8,128)(2,1)}) %all-gather.12.cloned.1.call-update) | async-done | bytes 4194320 | tf_op jit(solution)/shard_map/all_gather | solution.py:81
  159.1 6.5 copy.51
  165.6 26.1 %multiply_reduce_fusion = (f32[16,512]{1,0:T(8,128)S(1)}, f32[16,512,2048]{2,1,0:T(8,128)}) fusion(bf16[512,16,64]{0,2,1:T(8,128)(2,1)S(1)} %copy-done.2, bf16[2048,16,64]{0,2,1:T(8,128)(2,1)} %bitcast.118), kind=kOutput, calls=%fused_computation.7 | convolution fusion | flops 2181029888 | bytes 72384512 | tf_op jit(solution)/shard_map/qhd,khd->hqk/dot_general | solution.py:87
  191.7 48.9 %all-gather.14.cloned.1.call-done = bf16[2048,1024]{1,0:T(8,128)(2,1)} async-done(((bf16[512,1024]{1,0:T(8,128)(2,1)}), bf16[2048,1024]{1,0:T(8,128)(2,1)}) %all-gather.14.cloned.1.call-update) | async-done | bytes 4194320 | tf_op jit(solution)/shard_map/all_gather | solution.py:82
  240.6 6.5 copy.52
  247.1 21.9 %fusion = f32[16,512]{1,0:T(8,128)S(1)} fusion(f32[16,512,2048]{2,1,0:T(8,128)} %get-tuple-element.46, f32[16,512]{1,0:T(8,128)S(1)} %broadcast_maximum_fusion), kind=kLoop, calls=%fused_computation.4 | loop fusion | flops 50323456 | bytes 67174400 | tf_op jit(solution)/shard_map/reduce_sum | solution.py:92
  268.9 27.8 %fusion.72 = (bf16[512,16,64]{0,2,1:T(8,128)(2,1)}, f32[512,16,64]{0,2,1:T(8,128)}) fusion(f32[512,16]{0,1:T(8,128)S(1)} %bitcast.140, bf16[2048,16,64]{0,2,1:T(8,128)(2,1)} %bitcast.131, f32[16,512,2048]{2,1,0:T(8,128)} %get-tuple-element.46, f32[16,512]{1,0:T(8,128)S(1)} %broadcast_maximum_fusion), kind=kOutput, calls=%fused_computation.124 | convolution fusion | flops 2198863872 | bytes 74514432 | tf_op jit(solution)/shard_map/hqk,khd->hqd/dot_general | solution.py:93
  296.7 3.3 fusion.73
  300.4 34.5 %all-gather.18.cloned.1.call-done = bf16[1024,5248]{1,0:T(8,128)(2,1)} async-done(((bf16[128,5248]{1,0:T(8,128)(2,1)}), bf16[1024,5248]{1,0:T(8,128)(2,1)}) %all-gather.18.cloned.1.call-update) | async-done | bytes 10747920 | tf_op jit(solution)/shard_map/all_gather | solution.py:61
  334.9 12.8 %fusion.70 = f32[512,5248]{1,0:T(8,128)} fusion(bf16[1024,5248]{1,0:T(8,128)(2,1)} %all-gather.18.cloned.1.call-done, f32[512,1024]{1,0:T(8,128)S(1)} %get-tuple-element.50, f32[1024]{0:T(1024)S(1)} %bitcast.145, f32[512]{0:T(512)S(1)} %add_rsqrt_fusion, f32[512]{0:T(512)S(1)} %broadcast_multiply_fusion.6), kind=kOutput, calls=%fused_computation.122 | convolution fusion | flops 5505024000 | bytes 23601152 | tf_op jit(solution)/shard_map/dot_general | solution.py:107
  347.7 31.6 %all-gather.20.cloned.1.call-done = bf16[2624,1024]{1,0:T(8,128)(2,1)} async-done(((bf16[2624,128]{1,0:T(8,128)(2,1)}), bf16[2624,1024]{1,0:T(8,128)(2,1)}) %all-gather.20.cloned.1.call-update) | async-done | bytes 5373968 | tf_op jit(solution)/shard_map/all_gather | solution.py:62
  379.3 13.6 %fusion.20 = (bf16[512,2624]{1,0:T(8,128)(2,1)}, bf16[512,2624]{1,0:T(8,128)(2,1)}, bf16[512,2624]{1,0:T(8,128)(2,1)}) fusion(f32[512,5248]{1,0:T(8,128)} %fusion.70, bf16[2624,1024]{1,0:T(8,128)(2,1)} %all-gather.20.cloned.1.call-done, bf16[1,512,1024]{2,1,0:T(8,128)(2,1)S(1)} %copy-done.19), kind=kOutput, calls=%fused_computation.27 | convolution fusion | flops 2772959232 | bytes 25231360 | tf_op jit(solution)/shard_map/rd,fd->rf/dot_general | solution.py:131
  392.9 12.2 %multiply_reduce_fusion.1 = (bf16[1024]{0:T(1024)(128)(2,1)}, f32[512]{0:T(512)S(1)}, f32[512]{0:T(512)S(1)}, f32[512,1024]{1,0:T(8,128)S(1)}) fusion(f32[512,1024]{1,0:T(8,128)S(1)} %get-tuple-element.50, f32[512]{0:T(512)S(1)} %add_rsqrt_fusion, f32[512]{0:T(512)S(1)} %broadcast_multiply_fusion.6, f32[1024]{0:T(1024)S(1)} %bitcast.146, ...), kind=kOutput, calls=%fused_computation.71 | convolution fusion | flops 5517867008 | bytes 20330496 | tf_op jit(solution)/shard_map/rf,df->rd/dot_general | solution.py:138
  413.4 117.2 %all-gather.22.cloned.1.call-done = bf16[2048,2048]{1,0:T(8,128)(2,1)} async-done(((bf16[512,2048]{1,0:T(8,128)(2,1)}), bf16[2048,2048]{1,0:T(8,128)(2,1)}) %all-gather.22.cloned.1.call-update) | async-done | bytes 8388624 | tf_op jit(solution)/shard_map/all_gather | solution.py:188
  530.6 6.0 fusion.71
  536.6 6.6 copy.56
  543.2 25.5 %fusion.74 = f32[16,512,2048]{2,1,0:T(8,128)} fusion(bf16[512,16,64]{0,2,1:T(8,128)(2,1)S(1)} %copy-done.3, bf16[2048,16,64]{0,2,1:T(8,128)(2,1)} %bitcast.120), kind=kOutput, calls=%fused_computation.126 | convolution fusion | flops 2147483648 | bytes 72351744 | tf_op jit(solution)/shard_map/qhd,khd->hqk/dot_general | solution.py:167
  568.6 6.5 copy.57
  575.1 26.2 %fusion.21 = bf16[16,64,2048]{2,1,0:T(8,128)(2,1)} fusion(bf16[512,16,64]{0,2,1:T(8,128)(2,1)} %bitcast.124, f32[16,512,2048]{2,1,0:T(8,128)} %fusion.74, f32[16,512]{1,0:T(8,128)S(1)} %log_add_fusion), kind=kOutput, calls=%fused_computation.33 | convolution fusion | flops 2199912448 | bytes 72384512 | tf_op jit(solution)/shard_map/hqk,qhd->khd/dot_general | solution.py:197
  601.4 27.0 %multiply_convert_fusion.4 = bf16[16,64,2048]{2,1,0:T(8,128)(2,1)} fusion(bf16[512,16,64]{0,2,1:T(8,128)(2,1)S(1)} %copy-done.3, f32[16,512,2048]{2,1,0:T(8,128)} %fusion.74, f32[16,512]{1,0:T(8,128)S(1)} %fusion.46, f32[16,512]{1,0:T(8,128)S(1)} %log_add_fusion, bf16[512,16,64]{0,2,1:T(8,128)(2,1)} %bitcast.125, bf16[2048,16,64]{0,2,1:T(8,128)(2,1)} %bitcast.133), kind=kOutput, calls=%fused_computation.18 | convolution fusion | flops 4383047680 | bytes 77660160 | tf_op jit(solution)/shard_map/hqk,qhd->khd/dot_general | solution.py:194
  628.3 8.5 pad_maximum_fusion
  638.1 6.6 convolution_convert_fusion.1
  644.7 8.1 copy.67
  654.0 4.2 convolution_convert_fusion.3
  658.2 11.8 %convolution_convert_fusion = bf16[1024,5248]{1,0:T(8,128)(2,1)} fusion(bf16[512,2624]{1,0:T(8,128)(2,1)} %get-tuple-element.23, bf16[512,2624]{1,0:T(8,128)(2,1)} %get-tuple-element.22, f32[512,1024]{1,0:T(8,128)S(1)} %get-tuple-element.50, f32[1024]{0:T(1024)S(1)} %bitcast.148, f32[512]{0:T(512)S(1)} %add_rsqrt_fusion, f32[512]{0:T(512)S(1)} %broadcast_multiply_fusion.6), kind=kOutput, calls=%fused_computation.16 | convolution fusion | flops 5521145856 | bytes 18227200 | tf_op jit(solution)/shard_map/rd,rf->df/dot_general | solution.py:135
  671.3 32.7 %bitcast_multiply_fusion = (f32[512,16,64]{0,2,1:T(8,128)}, f32[16,64,512]{2,1,0:T(8,128)}) fusion(bf16[2048,16,64]{0,2,1:T(8,128)(2,1)} %bitcast.119, f32[16,512,2048]{2,1,0:T(8,128)} %get-tuple-element.46, f32[16,512]{1,0:T(8,128)S(1)} %fusion.46, f32[16,512]{1,0:T(8,128)S(1)} %log_add_fusion, bf16[512,16,64]{0,2,1:T(8,128)(2,1)S(1)} %bitcast.126, ...), kind=kOutput, calls=%fused_computation.66 | convolution fusion | flops 4379377664 | bytes 80805888 | tf_op jit(solution)/shard_map/hqk,khd->qhd/dot_general | solution.py:184
  704.0 2.8 slice_negate_fusion.1
  706.8 72.9 %reduce-scatter.8.cloned.1.call-done = bf16[512,2048]{0,1:T(8,128)(2,1)} async-done(((bf16[2048,2048]{0,1:T(8,128)(2,1)}), bf16[512,2048]{0,1:T(8,128)(2,1)}) %reduce-scatter.8.cloned.1.call-update) | async-done | bytes 2097168 | tf_op jit(solution)/shard_map/reduce_scatter | solution.py:203
  786.9 8.8 convolution_convert_fusion.2
  796.0 45.8 %reduce-scatter.16.cloned.1.call-done = bf16[128,2624]{1,0:T(8,128)(2,1)} async-done(((bf16[1024,2624]{1,0:T(8,128)(2,1)}), bf16[128,2624]{1,0:T(8,128)(2,1)}) %reduce-scatter.16.cloned.1.call-update) | async-done | bytes 671760
  844.0 42.5 %reduce-scatter.12.cloned.1.call-done = bf16[128,1024]{1,0:T(8,128)(2,1)} async-done(((bf16[1024,1024]{1,0:T(8,128)(2,1)}), bf16[128,1024]{1,0:T(8,128)(2,1)}) %reduce-scatter.12.cloned.1.call-update) | async-done | bytes 262160 | tf_op jit(solution)/shard_map/reduce_scatter | solution.py:225
  886.5 86.4 %reduce-scatter.14.cloned.1.call-done = bf16[128,5248]{1,0:T(8,128)(2,1)} async-done(((bf16[1024,5248]{1,0:T(8,128)(2,1)}), bf16[128,5248]{1,0:T(8,128)(2,1)}) %reduce-scatter.14.cloned.1.call-update) | async-done | bytes 1343504 | tf_op jit(solution)/shard_map/reduce_scatter | solution.py:144
  972.9 65.4 %reduce-scatter.10.cloned.1.call-done = bf16[128,3072]{1,0:T(8,128)(2,1)} async-done(((bf16[1024,3072]{1,0:T(8,128)(2,1)}), bf16[128,3072]{1,0:T(8,128)(2,1)}) %reduce-scatter.10.cloned.1.call-update) | async-done | bytes 786448 | tf_op jit(solution)/shard_map/reduce_scatter | solution.py:222
  1039.6 7.6 fusion.49
  1047.2 8.3 fusion.39
  1055.6 13.9 %all-reduce.2 = (bf16[1024]{0:T(1024)(128)(2,1)S(1)}, bf16[1024]{0:T(1024)(128)(2,1)S(1)}) all-reduce(bf16[1024]{0:T(1024)(128)(2,1)S(1)} %get-tuple-element.10, bf16[1024]{0:T(1024)(128)(2,1)S(1)} %copy-done.35), channel_id=7, replica_groups=mesh['fsdp'=8,'ctx'=4] {'fsdp'}, use_global_device_ids=true, to_apply=%region_20.0.clone | all-reduce | flops 2048 | bytes 8192
  1069.7 12.6 %all-reduce.3 = (bf16[128]{0:T(256)(128)(2,1)S(1)}, bf16[128]{0:T(256)(128)(2,1)S(1)}) all-reduce(bf16[128]{0:T(256)(128)(2,1)S(1)} %dynamic-slice.1, bf16[128]{0:T(256)(128)(2,1)S(1)} %dynamic-slice.3), channel_id=1, replica_groups=mesh['fsdp'=8,'ctx'=4] {'ctx'}, use_global_device_ids=true, to_apply=%region_21.0 | all-reduce | flops 256 | bytes 1024 | tf_op jit(solution)/shard_map/psum | solution.py:235
  1083.3 3.6 fusion.38
  1086.9 74.0 %all-reduce.7.cloned.1.call-done = (bf16[128,3072]{1,0:T(8,128)(2,1)}, bf16[128,1024]{1,0:T(8,128)(2,1)}, bf16[128,5248]{1,0:T(8,128)(2,1)}, bf16[2624,128]{1,0:T(8,128)(2,1)}) async-done(((bf16[128,3072]{1,0:T(8,128)(2,1)}, bf16[128,1024]{1,0:T(8,128)(2,1)}, bf16[128,5248]{1,0:T(8,128)(2,1)}, bf16[2624,128]{1,0:T(8,128)(2,1)}), (bf16[128,3072]{1,0:T(8,128)(2,1)}, bf16[128,1024]{1,0:T(8,128)(2,1)}, ...) | async-done | bytes 3063824 | tf_op jit(solution)/shard_map/psum | solution.py:233
  1160.8 3.1 convert_element_type.146
  (147 shorter events, 43.0 us)
Async XLA Ops:
  7.2 51.0 %all-gather.10.cloned.1.call-start = ((), (), s32[]{:S(2)}) async-start(), calls=%async_computation.5 | async-start | bytes 7077888 | tf_op jit(solution)/shard_map/all_gather | solution.py:59
  7.9 151.2 %all-gather.12.cloned.1.call-start = ((), (), s32[]{:S(2)}) async-start(), calls=%async_computation.6 | async-start | bytes 5242880 | tf_op jit(solution)/shard_map/all_gather | solution.py:81
  18.3 39.9 %copy-start.31 = (f32[8,1,128]{2,1,0:T(1,128)}, f32[8,1,128]{2,1,0:T(1,128)S(1)}, u32[]{:S(2)}) copy-start(f32[8,1,128]{2,1,0:T(1,128)S(1)} %convert_element_type.153) | copy-start | bytes 12292
  19.3 77.4 %copy-start.12 = (f32[512,64]{0,1:T(8,128)}, f32[512,64]{0,1:T(8,128)S(1)}, u32[]{:S(2)}) copy-start(f32[512,64]{0,1:T(8,128)S(1)} %get-tuple-element.44) | copy-start | bytes 393220
  19.3 2.1 copy-start
  21.6 42.3 %copy-start.29 = (f32[512]{0:T(512)}, f32[512]{0:T(512)S(1)}, u32[]{:S(2)}) copy-start(f32[512]{0:T(512)S(1)} %broadcast_multiply_fusion.7) | copy-start | bytes 6148
  22.1 41.8 %copy-start.33 = (f32[512]{0:T(512)}, f32[512]{0:T(512)S(1)}, u32[]{:S(2)}) copy-start(f32[512]{0:T(512)S(1)} %add_rsqrt_fusion.1) | copy-start | bytes 6148
  63.9 2.6 copy-start.6
  78.2 4.6 copy-start.36
  78.2 162.4 %all-gather.14.cloned.1.call-start = ((), (), s32[]{:S(2)}) async-start(), calls=%async_computation.7 | async-start | bytes 5242880 | tf_op jit(solution)/shard_map/all_gather | solution.py:82
  81.0 215.8 %all-gather.16.cloned.1.call-start = ((), (), s32[]{:S(2)}) async-start(), calls=%async_computation.8 | async-start | bytes 2359296 | tf_op jit(solution)/shard_map/all_gather | solution.py:60
  81.6 253.4 %all-gather.18.cloned.1.call-start = ((), (), s32[]{:S(2)}) async-start(), calls=%async_computation.9 | async-start | bytes 12091392 | tf_op jit(solution)/shard_map/all_gather | solution.py:61
  82.2 297.2 %all-gather.20.cloned.1.call-start = ((), (), s32[]{:S(2)}) async-start(), calls=%async_computation.10 | async-start | bytes 6045696 | tf_op jit(solution)/shard_map/all_gather | solution.py:62
  82.7 447.8 %all-gather.22.cloned.1.call-start = ((), (), s32[]{:S(2)}) async-start(), calls=%async_computation.11 | async-start | bytes 10485760 | tf_op jit(solution)/shard_map/all_gather | solution.py:188
  98.3 67.2 %copy-start.2 = (bf16[512,16,64]{0,2,1:T(8,128)(2,1)S(1)}, bf16[512,16,64]{0,2,1:T(8,128)(2,1)}, u32[]{:S(2)}) copy-start(bf16[512,16,64]{0,2,1:T(8,128)(2,1)} %fusion.42) | copy-start | bytes 3145732
  98.4 681.4 %reduce-scatter.8.cloned.1.call-start = ((), (), s32[]{:S(2)}) async-start(), calls=%async_computation.12 | async-start | bytes 10485760 | tf_op jit(solution)/shard_map/reduce_scatter | solution.py:203
  334.9 44.4 %copy-start.19 = (bf16[1,512,1024]{2,1,0:T(8,128)(2,1)S(1)}, bf16[1,512,1024]{2,1,0:T(8,128)(2,1)}, u32[]{:S(2)}) copy-start(bf16[1,512,1024]{2,1,0:T(8,128)(2,1)} %param.15) | copy-start | bytes 3145732
  405.1 2.1 copy-start.14
  405.9 1.3 copy-start.7
  411.0 125.6 %copy-start.4 = (bf16[512,1024]{0,1:T(8,128)(2,1)}, bf16[512,1024]{0,1:T(8,128)(2,1)S(1)}, u32[]{:S(2)}) copy-start(bf16[512,1024]{0,1:T(8,128)(2,1)S(1)} %copy.55) | copy-start | bytes 3145732
  536.6 6.6 copy-start.3
  636.9 204.9 %reduce-scatter.16.cloned.1.call-start = ((), (), s32[]{:S(2)}) async-start(), calls=%async_computation.16 | async-start | bytes 6193152
  652.7 1.2 copy-start.21
  652.8 233.8 %reduce-scatter.12.cloned.1.call-start = ((), (), s32[]{:S(2)}) async-start(), calls=%async_computation.14 | async-start | bytes 2359296 | tf_op jit(solution)/shard_map/reduce_scatter | solution.py:225
  658.2 314.7 %reduce-scatter.14.cloned.1.call-start = ((), (), s32[]{:S(2)}) async-start(), calls=%async_computation.15 | async-start | bytes 12091392 | tf_op jit(solution)/shard_map/reduce_scatter | solution.py:144
  670.0 1.3 copy-start.5
  670.1 368.2 %reduce-scatter.10.cloned.1.call-start = ((), (), s32[]{:S(2)}) async-start(), calls=%async_computation.13 | async-start | bytes 7077888 | tf_op jit(solution)/shard_map/reduce_scatter | solution.py:222
  781.6 4.3 copy-start.15
  781.6 1.6 copy-start.10
  781.6 2.3 copy-start.11
  781.7 2.3 copy-start.26
  781.7 2.3 copy-start.27
  783.9 1.6 copy-start.9
  783.9 1.6 copy-start.13
  784.9 2.0 copy-start.1
  784.9 2.0 copy-start.30
  784.9 2.0 copy-start.32
  784.9 2.0 copy-start.34
  795.7 242.6 %copy-start.37 = (u32[32]{0:T(128)S(1)}, u32[32]{0:T(128)}, u32[]{:S(2)}) copy-start(u32[32]{0:T(128)} %constant.50) | copy-start | bytes 388
  795.7 365.1 %all-reduce.7.cloned.1.call-start = ((), (), s32[]{:S(2)}) async-start(), calls=%async_computation.17 | async-start | bytes 6127616 | tf_op jit(solution)/shard_map/psum | solution.py:233
  1039.5 7.7 copy-start.16
  1039.6 7.6 copy-start.18
  1039.6 7.6 copy-start.23
  1047.2 8.4 copy-start.35
  1047.2 36.1 %copy-start.8 = (f32[512,1024]{1,0:T(8,128)S(1)}, f32[512,1024]{1,0:T(8,128)}, u32[]{:S(2)}) copy-start(f32[512,1024]{1,0:T(8,128)} %copy-done.7) | copy-start | bytes 6291460
  1160.8 3.1 copy-start.24
  1160.8 4.4 copy-start.25
  1164.0 2.5 copy-start.28
  (3 other events, 3.3 us)
Sparse Core Ops, SparseCore 0:
  9.9 48.2 all-gather.9
  78.3 80.7 all-gather.11
  161.2 79.2 all-gather.13
  242.3 26.4 all-gather.15
  270.5 64.3 all-gather.17
  336.7 42.6 all-gather.19
  380.9 149.6 all-gather.21
  637.0 142.6 reduce-scatter.7
  783.2 58.5 reduce-scatter.15
  845.3 41.2 reduce-scatter.11
  890.1 82.7 reduce-scatter.13
  976.5 61.7 reduce-scatter.9
  1040.9 119.8 all-reduce.6
where the time goes:
time: 1180 us; the launch traced here: 1170 us
  waiting for transfers between devices  718 us (61%)
  matrix products  262 us (22%)
  local copies, waits for them, and re-layouts  67.5 us (6%)
  other arithmetic  64.3 us (5%)
  blocking collectives  45.5 us (4%)
  between operations  15.4 us (1%)
    all_gather x1, waiting for transfers between devices, local(): piece = lax.all_gather(key_value_rows, 'ctx', axis=0, tiled=True)  117 us
    reduce_scatter x1, waiting for transfers between devices, local(): lax.psum_scatter(grad_win.astype(jnp.bfloat16), 'fsdp', scatter_dimension...  86.4 us
    psum x1, waiting for transfers between devices, local(): lax.psum(attn_parts[0].astype(jnp.bfloat16), 'ctx').astype(jnp.float32)  74 us
    reduce_scatter x1, waiting for transfers between devices, local(): lax.psum_scatter(grad_kv.astype(jnp.bfloat16), 'ctx', scatter_dimension=0...  72.9 us
    reduce_scatter x1, waiting for transfers between devices, local(): lax.psum_scatter(grad_wqkv.astype(jnp.bfloat16), 'fsdp', scatter_dimensio...  65.4 us
    all_gather x1, waiting for transfers between devices, local(): key_block = lax.all_gather(keys, 'ctx', axis=0, tiled=True)  60.5 us
    all_gather x1, waiting for transfers between devices, local(): value_block = lax.all_gather(values, 'ctx', axis=0, tiled=True)  48.9 us
    unnamed x14, waiting for transfers between devices  48.2 us
  transfers between devices with their start and end apart: 13, of which 12 were waited for; matrix products, arithmetic and copies ran while one was open for 22% of the time, Pallas kernels for 0%

commit v1 on v0

v1 whole, which is shorter than its diff:
```python
import math

import jax
import jax.numpy as jnp
from jax import lax
from jax.experimental import pallas as pl
from jax.experimental.pallas import tpu as pltpu
from jax.sharding import PartitionSpec as P

HEADS = 16
HEAD_DIM = 64


EPSILON = 1e-05
ROPE_BASE = 160000.0


def normalize(values):
    row_mean = jnp.mean(values, -1, keepdims=True)
    centered = values - row_mean
    variance = jnp.mean(centered * centered, -1, keepdims=True)
    inv_std = lax.rsqrt(variance + EPSILON)
    return (centered * inv_std, inv_std)


def norm_back(grad_normed, normed, inv_std):
    first_mean = jnp.mean(grad_normed, -1, keepdims=True)
    second_mean = jnp.mean(grad_normed * normed, -1, keepdims=True)
    return inv_std * (grad_normed - first_mean - normed * second_mean)


def rope_tables(first_row, local_rows):
    positions = (first_row + jnp.arange(local_rows, dtype=jnp.int32)).astype(jnp.float32)
    inv_freq = ROPE_BASE ** (-(jnp.arange(HEAD_DIM // 2, dtype=jnp.float32) * 2.0 / HEAD_DIM))
    angles = positions[:, None] * inv_freq[None, :]
    angles = jnp.concatenate([angles, angles], -1)
    return (jnp.cos(angles)[:, None, :], jnp.sin(angles)[:, None, :])


def rotate(vectors, cosine, sine):
    half_dim = vectors.shape[-1] // 2
    turned = jnp.concatenate([-vectors[..., half_dim:], vectors[..., :half_dim]], -1)
    return vectors * cosine + turned * sine


def dot_rows(left, right):
    return lax.dot_general(
        left, right, (((1,), (1,)), ((), ())), preferred_element_type=jnp.float32
    )


def only_head(block, head):
    if block.shape[1] == HEAD_DIM:
        return block
    lane = lax.broadcasted_iota(jnp.int32, block.shape, 1)
    inside = (lane >= head * HEAD_DIM) & (lane < (head + 1) * HEAD_DIM)
    return jnp.where(inside, block.astype(jnp.float32), 0.0).astype(jnp.bfloat16)


def attend_kernel(q_ref, k_ref, v_ref, o_ref, lse_ref, vt_ref):
    @pl.when(pl.program_id(1) == 0)
    def _():
        vt_ref[...] = v_ref[...].T

    results = []
    for head in range(q_ref.shape[1] // HEAD_DIM):
        rows = slice(head * HEAD_DIM, (head + 1) * HEAD_DIM)
        scores = dot_rows(k_ref[...], only_head(q_ref[...], head))
        peak = jnp.max(scores, 0, keepdims=True)
        weights = jnp.exp(scores - peak)
        total = jnp.sum(weights, 0, keepdims=True)
        summed = jnp.dot(
            vt_ref[rows, :], weights.astype(jnp.bfloat16), preferred_element_type=jnp.float32
        )
        results.append(summed / total)
        lse_ref[0, head : head + 1, :] = peak + jnp.log(total)
    o_ref[...] = jnp.concatenate(results, 0).T


def attend_back_kernel(
    q_ref, k_ref, v_ref, o_ref, lse_ref, g_ref, dq_ref, dk_ref, dv_ref, kt_ref, dk_sum, dv_sum
):
    @pl.when(pl.program_id(1) == 0)
    def _():
        kt_ref[...] = k_ref[...].T
        dk_sum[...] = jnp.zeros_like(dk_sum)
        dv_sum[...] = jnp.zeros_like(dv_sum)

    products = (g_ref[...].astype(jnp.float32) * o_ref[...]).T
    results = []
    for head in range(q_ref.shape[1] // HEAD_DIM):
        rows = slice(head * HEAD_DIM, (head + 1) * HEAD_DIM)
        query = only_head(q_ref[...], head)
        grad = only_head(g_ref[...], head)
        probs = jnp.exp(dot_rows(k_ref[...], query) - lse_ref[0, head : head + 1, :])
        delta = jnp.sum(products[rows, :], 0, keepdims=True)
        grad_probs = dot_rows(v_ref[...], grad)
        grad_scores = (probs * (grad_probs - delta)).astype(jnp.bfloat16)
        dv_sum[...] += jnp.dot(
            probs.astype(jnp.bfloat16), grad, preferred_element_type=jnp.float32
        )
        dk_sum[...] += jnp.dot(grad_scores, query, preferred_element_type=jnp.float32)
        results.append(jnp.dot(kt_ref[rows, :], grad_scores, preferred_element_type=jnp.float32))
    dq_ref[...] = (jnp.concatenate(results, 0) * HEAD_DIM**-0.5).T.astype(jnp.bfloat16)

    @pl.when(pl.program_id(1) == pl.num_programs(1) - 1)
    def _():
        dk_ref[...] = dk_sum[...].astype(jnp.bfloat16)
        dv_ref[...] = dv_sum[...].astype(jnp.bfloat16)


def kernel_plan(packed):
    total_rows, width = packed.shape[0], packed.shape[1] // 3
    block_width = 2 * HEAD_DIM if width % (2 * HEAD_DIM) == 0 else width
    groups = width // block_width
    block_rows = min(256, total_rows)
    by_rows = pl.BlockSpec((block_rows, block_width), lambda g, r: (r, g))
    hop = groups if block_width % 128 == 0 else 0
    column = [
        pl.BlockSpec((block_rows, block_width), lambda g, r: (r, g)),
        pl.BlockSpec((total_rows, block_width), lambda g, r: (0, hop + g)),
        pl.BlockSpec((total_rows, block_width), lambda g, r: (0, 2 * hop + g)),
    ]
    heads = block_width // HEAD_DIM
    lse_spec = pl.BlockSpec((1, heads, block_rows), lambda g, r: (g, 0, r))
    lse_shape = jax.ShapeDtypeStruct((groups, heads, total_rows), jnp.float32)
    grid = (groups, total_rows // block_rows)
    params = pltpu.CompilerParams(vmem_limit_bytes=48 * 1024 * 1024)
    return total_rows, width, block_width, by_rows, column, lse_spec, lse_shape, grid, params


def thirds(packed):
    width = packed.shape[1] // 3
    if width % 128 == 0:
        return (packed, packed, packed)
    return tuple(packed[:, part * width : (part + 1) * width] for part in range(3))


def attend(packed):
    total_rows, width, block_width, by_rows, column, lse_spec, lse_shape, grid, params = (
        kernel_plan(packed)
    )
    work = HEAD_DIM * total_rows * total_rows * (width // HEAD_DIM)
    return pl.pallas_call(
        attend_kernel,
        grid=grid,
        in_specs=column,
        out_specs=(by_rows, lse_spec),
        out_shape=(jax.ShapeDtypeStruct((total_rows, width), jnp.float32), lse_shape),
        scratch_shapes=[pltpu.VMEM((block_width, total_rows), jnp.bfloat16)],
        compiler_params=params,
        cost_estimate=pl.CostEstimate(
            flops=8 * work, bytes_accessed=10 * total_rows * width, transcendentals=work // HEAD_DIM
        ),
    )(*thirds(packed))


def attend_back(packed, attended, log_total, grad):
    total_rows, width, block_width, by_rows, column, lse_spec, lse_shape, grid, params = (
        kernel_plan(packed)
    )
    whole = pl.BlockSpec((total_rows, block_width), lambda g, r: (0, g))
    low_shape = jax.ShapeDtypeStruct((total_rows, width), jnp.bfloat16)
    work = HEAD_DIM * total_rows * total_rows * (width // HEAD_DIM)
    return pl.pallas_call(
        attend_back_kernel,
        grid=grid,
        in_specs=column + [by_rows, lse_spec, by_rows],
        out_specs=(by_rows, whole, whole),
        out_shape=(low_shape, low_shape, low_shape),
        scratch_shapes=[
            pltpu.VMEM((block_width, total_rows), jnp.bfloat16),
            pltpu.VMEM((total_rows, block_width), jnp.float32),
            pltpu.VMEM((total_rows, block_width), jnp.float32),
        ],
        compiler_params=params,
        cost_estimate=pl.CostEstimate(
            flops=20 * work, bytes_accessed=20 * total_rows * width, transcendentals=work // HEAD_DIM
        ),
    )(*thirds(packed), attended, log_total, grad)


def to_heads(arrays):
    count, me = lax.axis_size("ctx"), lax.axis_index("ctx")
    width = arrays[0].shape[1] // count
    received = []
    for step in range(count):
        start = lax.rem(me + step, count) * width
        piece = jnp.concatenate(
            [lax.dynamic_slice_in_dim(item, start, width, 1) for item in arrays], 1
        )
        if step:
            piece = lax.ppermute(
                piece, "ctx", [(source, (source + step) % count) for source in range(count)]
            )
        received.append(piece)
    return jnp.concatenate(received, 0)


def to_rows(arrays):
    count, me = lax.axis_size("ctx"), lax.axis_index("ctx")
    rows, width = arrays[0].shape[0] // count, arrays[0].shape[1]
    received = []
    for step in range(count):
        piece = jnp.concatenate([item[step * rows : (step + 1) * rows] for item in arrays], 1)
        if step:
            piece = lax.ppermute(
                piece, "ctx", [(source, (source - step) % count) for source in range(count)]
            )
        received.append(piece)
    start = lax.rem(count - me, count) * width
    results = []
    for number in range(len(arrays)):
        turned = [item[:, number * width : (number + 1) * width] for item in received]
        doubled = jnp.concatenate(turned + turned, 1)
        results.append(lax.dynamic_slice_in_dim(doubled, start, count * width, 1))
    return results


def local(
    tokens,
    query_key_value_weight,
    attention_output_weight,
    geglu_input_weight,
    geglu_output_weight,
    gain_one,
    gain_two,
    cotangent,
):
    local_rows = tokens.shape[1]
    model_width = tokens.shape[2]
    hidden_width = geglu_output_weight.shape[0]
    score_scale = HEAD_DIM ** (-0.5)
    full_qkv, full_attn, full_in, full_out, full_one, full_two = (
        lax.all_gather(query_key_value_weight, "fsdp", axis=0, tiled=True),
        lax.all_gather(attention_output_weight, "fsdp", axis=0, tiled=True),
        lax.all_gather(geglu_input_weight, "fsdp", axis=0, tiled=True),
        lax.all_gather(geglu_output_weight, "fsdp", axis=1, tiled=True),
        *lax.all_gather(jnp.stack([gain_one, gain_two]), "fsdp", axis=1, tiled=True),
    )
    inputs = tokens[0].astype(jnp.float32)
    normed_one, inv_one = normalize(inputs)
    hidden_after_attention = (normed_one * full_one.astype(jnp.float32)).astype(jnp.bfloat16)
    query_key_value = jnp.dot(hidden_after_attention, full_qkv, preferred_element_type=jnp.float32)
    cosine, sine = rope_tables(lax.axis_index("ctx") * local_rows, local_rows)
    head_shape = (local_rows, HEADS, HEAD_DIM)
    query = rotate(query_key_value[:, :model_width].reshape(head_shape), cosine, sine)
    query = (query.astype(jnp.bfloat16) * score_scale).reshape(local_rows, model_width)
    keys = rotate(
        query_key_value[:, model_width : 2 * model_width].reshape(head_shape), cosine, sine
    ).astype(jnp.bfloat16)
    keys = keys.reshape(local_rows, model_width)
    values = query_key_value[:, 2 * model_width :].astype(jnp.bfloat16)
    packed = to_heads((query, keys, values))
    attended, log_total = attend(packed)
    (attn_low,) = to_rows((attended.astype(jnp.bfloat16),))
    middle_activation = inputs + jnp.dot(attn_low, full_attn, preferred_element_type=jnp.float32)
    normed_two, inv_two = normalize(middle_activation)
    hidden_after_feedforward = (normed_two * full_two.astype(jnp.float32)).astype(jnp.bfloat16)
    projected_up_rows = jnp.dot(
        hidden_after_feedforward, full_in, preferred_element_type=jnp.float32
    )
    gate_in = projected_up_rows[:, :hidden_width]
    gate_up = projected_up_rows[:, hidden_width:]
    normal_cdf = 0.5 * (1.0 + lax.erf(gate_in * (1.0 / math.sqrt(2.0))))
    normal_pdf = jnp.exp(-0.5 * gate_in * gate_in) * (1.0 / math.sqrt(2.0 * math.pi))
    activated = gate_in * normal_cdf
    hidden_state = (activated * gate_up).astype(jnp.bfloat16)
    mixed = (
        middle_activation + jnp.dot(hidden_state, full_out, preferred_element_type=jnp.float32)
    ).astype(jnp.bfloat16)
    back_qkv, back_attn, back_in, back_out, back_one, back_two = (
        full_qkv,
        full_attn,
        full_in,
        full_out,
        full_one,
        full_two,
    )
    grad_mixed = cotangent[0]
    grad_wout = jnp.einsum(
        "rf,rd->fd", hidden_state, grad_mixed, preferred_element_type=jnp.float32
    )
    grad_hidden = jnp.einsum("rd,fd->rf", grad_mixed, back_out, preferred_element_type=jnp.float32)
    grad_up = jnp.concatenate(
        [grad_hidden * gate_up * (normal_cdf + gate_in * normal_pdf), grad_hidden * activated], -1
    ).astype(jnp.bfloat16)
    grad_win = jnp.einsum(
        "rd,rf->df", hidden_after_feedforward, grad_up, preferred_element_type=jnp.float32
    )
    grad_htwo = jnp.einsum("rf,df->rd", grad_up, back_in, preferred_element_type=jnp.float32)
    grad_two = jnp.sum(grad_htwo * normed_two, 0)
    grad_middle = grad_mixed.astype(jnp.float32) + norm_back(
        grad_htwo * back_two.astype(jnp.float32), normed_two, inv_two
    )
    part_win = lax.psum_scatter(
        grad_win.astype(jnp.bfloat16), "fsdp", scatter_dimension=0, tiled=True
    )
    part_wout = lax.psum_scatter(
        grad_wout.astype(jnp.bfloat16), "fsdp", scatter_dimension=1, tiled=True
    )
    sum_win, sum_wout = lax.psum((part_win, part_wout), "ctx")
    grad_branch = grad_middle.astype(jnp.bfloat16)
    grad_wattn = jnp.einsum("rd,re->de", attn_low, grad_branch, preferred_element_type=jnp.float32)
    grad_attn = jnp.einsum("re,de->rd", grad_branch, back_attn, preferred_element_type=jnp.float32)
    (grad_heads,) = (to_heads((grad_attn.astype(jnp.bfloat16),)),)
    back_query, back_keys, grad_v = to_rows(attend_back(packed, attended, log_total, grad_heads))
    grad_q = rotate(back_query.reshape(head_shape).astype(jnp.float32), cosine, -sine)
    grad_k = rotate(back_keys.reshape(head_shape).astype(jnp.float32), cosine, -sine)
    grad_qkv_rows = jnp.concatenate(
        [
            grad_q.reshape(local_rows, model_width).astype(jnp.bfloat16),
            grad_k.reshape(local_rows, model_width).astype(jnp.bfloat16),
            grad_v,
        ],
        -1,
    )
    grad_wqkv = jnp.einsum(
        "rd,re->de", hidden_after_attention, grad_qkv_rows, preferred_element_type=jnp.float32
    )
    grad_hone = jnp.einsum("re,de->rd", grad_qkv_rows, back_qkv, preferred_element_type=jnp.float32)
    grad_one = jnp.sum(grad_hone * normed_one, 0)
    grad_inputs = grad_middle + norm_back(
        grad_hone * back_one.astype(jnp.float32), normed_one, inv_one
    )
    part_wqkv = lax.psum_scatter(
        grad_wqkv.astype(jnp.bfloat16), "fsdp", scatter_dimension=0, tiled=True
    )
    part_wattn = lax.psum_scatter(
        grad_wattn.astype(jnp.bfloat16), "fsdp", scatter_dimension=0, tiled=True
    )
    sum_win, sum_wout, part_wqkv, part_wattn = lax.optimization_barrier(
        (sum_win, sum_wout, part_wqkv, part_wattn)
    )
    sum_wqkv, sum_wattn = lax.psum((part_wqkv, part_wattn), "ctx")
    sum_win, sum_wout, sum_wqkv, sum_wattn = (
        item.astype(jnp.float32) for item in (sum_win, sum_wout, sum_wqkv, sum_wattn)
    )
    gains = lax.psum(jnp.stack([grad_one, grad_two]), ("fsdp", "ctx"))
    shard = gain_one.shape[0]
    gains = lax.dynamic_slice_in_dim(gains, lax.axis_index("fsdp") * shard, shard, 1)
    sum_one, sum_two = gains[0], gains[1]
    return (
        mixed[None],
        grad_inputs[None],
        sum_wqkv,
        sum_wattn,
        sum_win,
        sum_wout,
        sum_one,
        sum_two,
    )


def solution(mesh):
    placed = (
        P("fsdp", "ctx", None),
        P("fsdp", None),
        P("fsdp", None),
        P("fsdp", None),
        P(None, "fsdp"),
        P("fsdp"),
        P("fsdp"),
        P("fsdp", "ctx", None),
    )
    return jax.shard_map(
        local,
        mesh=mesh,
        in_specs=placed,
        out_specs=(
            P("fsdp", "ctx", None),
            P("fsdp", "ctx", None),
            P("fsdp", None),
            P("fsdp", None),
            P("fsdp", None),
            P(None, "fsdp"),
            P("fsdp"),
            P("fsdp"),
        ),
        check_vma=False,
    )
```

time: 1180 us -> 733 us (0.62)
  waiting for transfers between devices: 718 us -> 324 us
  matrix products: 262 us -> 89.6 us
  Pallas kernels: 0 us -> 91.7 us
  starting transfers between devices: 0.99 us -> 33 us
  other arithmetic: 64.3 us -> 45.8 us
    all_gather x3 -> x0, waiting for transfers between devices: 227 us -> none  [the longest x1 117 us: local(): piece = lax.all_gather(key_value_rows, 'ctx', axis=0, tiled=True)]
    dot_general x6 -> x0, matrix products: 165 us -> none  [the longest x1 32.7 us: local(): jnp.einsum('hqk,khd->qhd', grad_scores, key_heads, preferred_element_type...]
    ppermute x0 -> x12, waiting for transfers between devices: none -> 153 us  [the longest x6 82.6 us: to_rows(): lax.ppermute(piece, 'ctx', [(source, (source - step) % count) for source...]
    pallas_call x0 -> x2, Pallas kernels: none -> 91.7 us  [the longest x1 48.2 us: attend_back(): pl.pallas_call(attend_back_kernel, grid=grid, in_specs=column + [by_rows,...]
    reduce_scatter x1, waiting for transfers between devices: 86.4 us -> 0.01 us  [local(): lax.psum_scatter(grad_win.astype(jnp.bfloat16), 'fsdp', scatter_dimension...]
    reduce_scatter x1 -> x0, waiting for transfers between devices: 72.9 us -> none  [local(): lax.psum_scatter(grad_kv.astype(jnp.bfloat16), 'ctx', scatter_dimension=0...]
    reduce_scatter x1, waiting for transfers between devices: 65.4 us -> 2.76 us  [local(): lax.psum_scatter(grad_wqkv.astype(jnp.bfloat16), 'fsdp', scatter_dimensio...]
    psum x1 -> x2, waiting for transfers between devices: 74 us -> 133 us  [the longest x1 86.8 us: local(): sum_win, sum_wout = lax.psum((part_win, part_wout), 'ctx')]
  transfers between devices with their start and end apart: 13 -> 22, of which waited for: 12 -> 12; matrix products, arithmetic and copies ran while one was open for 22% -> 24% of each run, Pallas kernels for 0% -> 13%
where the time goes in v1:
time: 733 us; the launch traced here: 726 us
  waiting for transfers between devices  324 us (44%)
  Pallas kernels  91.7 us (13%)
  matrix products  89.6 us (12%)
  local copies, waits for them, and re-layouts  78.2 us (11%)
  blocking collectives  48.1 us (7%)
  other arithmetic  45.8 us (6%)
  starting transfers between devices  33 us (5%)
  between operations  15 us (2%)
    psum x1, waiting for transfers between devices, local(): sum_win, sum_wout = lax.psum((part_win, part_wout), 'ctx')  86.8 us
    ppermute x6, waiting for transfers between devices, to_rows(): lax.ppermute(piece, 'ctx', [(source, (source - step) % count) for source...  82.6 us
    ppermute x6, waiting for transfers between devices, to_heads(): lax.ppermute(piece, 'ctx', [(source, (source + step) % count) for source...  70.3 us
    pallas_call x1, Pallas kernels, attend_back(): pl.pallas_call(attend_back_kernel, grid=grid, in_specs=column + [by_rows,...  48.2 us
    psum x1, waiting for transfers between devices, local(): sum_wqkv, sum_wattn = lax.psum((part_wqkv, part_wattn), 'ctx')  45.8 us
    pallas_call x1, Pallas kernels, attend(): pl.pallas_call(attend_kernel, grid=grid, in_specs=column, out_specs=(by_r...  43.5 us
    unnamed x78, local copies, waits for them, and re-layouts  41.6 us
    psum x1, blocking collectives, local(): gains = lax.psum(jnp.stack([grad_one, grad_two]), ('fsdp', 'ctx'))  37.9 us
  transfers between devices with their start and end apart: 22, of which 12 were waited for; matrix products, arithmetic and copies ran while one was open for 24% of the time, Pallas kernels for 13%

profile of v1, /device:TPU:0, one launch (start us, length us, event | category | flops | bytes accessed | tf_op | source)
XLA Modules:
  0.0 725.7 jit_solution(12990637323499916992)
XLA Ops:
  10.8 10.2 %all_gather.15 = bf16[2,1024]{1,0:T(2,128)(2,1)S(1)} all-gather(bf16[2,128]{1,0:T(2,128)(2,1)S(1)} %pad_maximum_fusion.16), channel_id=1, replica_groups=mesh['fsdp'=8,'ctx'=4] {'fsdp'}, dimensions={1}, use_global_device_ids=true | all-gather | bytes 4608 | tf_op jit(solution)/shard_map/all_gather | solution.py:239
  24.9 33.3 %all-gather.5.cloned.1.call-done = bf16[1024,3072]{1,0:T(8,128)(2,1)} async-done(((bf16[128,3072]{1,0:T(8,128)(2,1)}), bf16[1024,3072]{1,0:T(8,128)(2,1)}) %all-gather.5.cloned.1.call-update) | async-done | bytes 6291472 | tf_op jit(solution)/shard_map/all_gather | solution.py:235
  58.2 5.7 fusion.43
  63.9 2.7 copy-done.4
  68.0 2.9 copy.36
  74.2 2.9 copy.37
  77.1 5.6 fusion.46
  82.7 2.9 copy.33
  89.0 2.9 copy.34
  93.8 3.1 fusion.25
  98.8 2.5 collective-permute-start.1
  103.0 16.5 %collective-permute-done = bf16[512,768]{1,0:T(8,128)(2,1)S(1)} collective-permute-done((bf16[512,768]{1,0:T(8,128)(2,1)S(1)}, bf16[512,768]{1,0:T(8,128)(2,1)S(1)}, u32[]{:S(2)}, u32[]{:S(2)}) %collective-permute-start) | collective-permute-done | bytes 786464 | tf_op jit(solution)/shard_map/ppermute | solution.py:193
  119.6 33.0 %collective-permute-done.1 = bf16[512,768]{1,0:T(8,128)(2,1)S(1)} collective-permute-done((bf16[512,768]{1,0:T(8,128)(2,1)S(1)}, bf16[512,768]{1,0:T(8,128)(2,1)S(1)}, u32[]{:S(2)}, u32[]{:S(2)}) %collective-permute-start.1) | collective-permute-done | bytes 786464 | tf_op jit(solution)/shard_map/ppermute | solution.py:193
  152.6 3.3 pad_maximum_fusion.3.q_ref.k_ref.v_ref
  155.9 43.5 %shard_map.143 = (f32[2048,256]{1,0:T(8,128)S(1)}, f32[2,2,2048]{2,1,0:T(2,128)S(1)}) custom-call(bf16[2048,768]{1,0:T(8,128)(2,1)S(1)} %pad_maximum_fusion.3.q_ref.k_ref.v_ref, bf16[2048,768]{1,0:T(8,128)(2,1)S(1)} %pad_maximum_fusion.3.q_ref.k_ref.v_ref, bf16[2048,768]{1,0:T(8,128)(2,1)S(1)} %pad_maximum_fusion.3.q_ref.k_ref.v_ref), custom_call_target="tpu_custom_call" | custom-call | flops 8589934592 | bytes 5242880 | tf_op jit(solution)/shard_map/pallas_call | solution.py:144
  201.0 18.2 %collective-permute-start.3 = (bf16[512,256]{1,0:T(8,128)(2,1)}, bf16[512,256]{1,0:T(8,128)(2,1)S(1)}, u32[]{:S(2)}, u32[]{:S(2)}) collective-permute-start(bf16[512,256]{1,0:T(8,128)(2,1)} %get-tuple-element.72), channel_id=1, source_target_pairs={{0,3},{1,0},{2,1},{3,2},{4,7},{5,4},{6,5},{7,6},{8,11},{9,8},{10,9... | collective-permute-start | bytes 786440 | tf_op jit(solution)/shard_map/ppermute | solution.py:207
  220.0 6.3 collective-permute-done.3
  227.1 16.1 %collective-permute-done.4 = bf16[512,256]{1,0:T(8,128)(2,1)S(1)} collective-permute-done((bf16[512,256]{1,0:T(8,128)(2,1)}, bf16[512,256]{1,0:T(8,128)(2,1)S(1)}, u32[]{:S(2)}, u32[]{:S(2)}) %collective-permute-start.4) | collective-permute-done | bytes 262176 | tf_op jit(solution)/shard_map/ppermute | solution.py:207
  247.5 3.3 fusion.49
  251.1 13.1 %fusion.45 = f32[512,5248]{1,0:T(8,128)} fusion(bf16[1024,5248]{1,0:T(8,128)(2,1)} %all-gather.9.cloned.1.call-done, f32[512,1024]{1,0:T(8,128)S(1)} %get-tuple-element.110, f32[1024]{0:T(1024)S(1)} %bitcast.94, f32[512]{0:T(512)S(1)} %add_rsqrt_fusion, f32[512]{0:T(512)S(1)} %broadcast_multiply_fusion.5), kind=kOutput, calls=%fused_computation.157 | convolution fusion | flops 5505024000 | bytes 23601152 | tf_op jit(solution)/shard_map/dot_general | solution.py:260
  264.3 12.8 %fusion.5 = (bf16[512,2624]{1,0:T(8,128)(2,1)}, bf16[512,2624]{1,0:T(8,128)(2,1)}, bf16[512,2624]{1,0:T(8,128)(2,1)S(1)}) fusion(f32[512,5248]{1,0:T(8,128)} %fusion.45, bf16[2624,1024]{1,0:T(8,128)(2,1)} %all-gather.11.cloned.1.call-done, bf16[1,512,1024]{2,1,0:T(8,128)(2,1)S(1)} %copy-done.18), kind=kOutput, calls=%fused_computation.9 | convolution fusion | flops 2772959232 | bytes 25231360 | tf_op jit(solution)/shard_map/rd,fd->rf/dot_general | solution.py:284
  278.6 4.8 convolution_convert_fusion.2
  283.4 7.9 %copy.47 = bf16[2624,1024]{0,1:T(8,128)(2,1)} copy(bf16[2624,1024]{1,0:T(8,128)(2,1)} %convolution_convert_fusion.2) | data formatting | bytes 10747904
  291.4 11.7 %convolution_convert_fusion = bf16[1024,5248]{1,0:T(8,128)(2,1)} fusion(bf16[512,2624]{1,0:T(8,128)(2,1)} %get-tuple-element.37, bf16[512,2624]{1,0:T(8,128)(2,1)} %get-tuple-element.36, f32[512,1024]{1,0:T(8,128)S(1)} %get-tuple-element.110, f32[1024]{0:T(1024)S(1)} %bitcast.95, f32[512]{0:T(512)S(1)} %add_rsqrt_fusion, f32[512]{0:T(512)S(1)} %broadcast_multiply_fusion.5), kind=kOutput, calls=%fused_computation | convolution fusion | flops 5521145856 | bytes 18227200 | tf_op jit(solution)/shard_map/rd,rf->df/dot_general | solution.py:288
  303.7 11.4 %multiply_reduce_fusion = (f32[1024]{0:T(1024)S(1)}, f32[512]{0:T(512)S(1)}, f32[512]{0:T(512)S(1)}, f32[512,1024]{1,0:T(8,128)S(1)}) fusion(f32[512,1024]{1,0:T(8,128)S(1)} %get-tuple-element.110, f32[512]{0:T(512)S(1)} %add_rsqrt_fusion, f32[512]{0:T(512)S(1)} %broadcast_multiply_fusion.5, f32[1024]{0:T(1024)S(1)} %bitcast.96, ...), kind=kOutput, calls=%fused_computation.41 | convolution fusion | flops 5517867008 | bytes 20332544 | tf_op jit(solution)/shard_map/rf,df->rd/dot_general | solution.py:291
  321.0 6.0 collective-permute-done.8
  327.0 14.8 %collective-permute-done.7 = bf16[512,256]{1,0:T(8,128)(2,1)S(1)} collective-permute-done((bf16[512,256]{1,0:T(8,128)(2,1)S(1)}, bf16[512,256]{1,0:T(8,128)(2,1)S(1)}, u32[]{:S(2)}, u32[]{:S(2)}) %collective-permute-start.7) | collective-permute-done | bytes 262176 | tf_op jit(solution)/shard_map/ppermute | solution.py:193
  341.9 48.2 %shard_map.144 = (bf16[2048,256]{1,0:T(8,128)(2,1)S(1)}, bf16[2048,256]{1,0:T(8,128)(2,1)S(1)}, bf16[2048,256]{1,0:T(8,128)(2,1)S(1)}) custom-call(bf16[2048,768]{1,0:T(8,128)(2,1)} %copy-done, bf16[2048,768]{1,0:T(8,128)(2,1)} %copy-done, bf16[2048,768]{1,0:T(8,128)(2,1)} %copy-done, f32[2048,256]{1,0:T(8,128)} %copy-done.1, ...), custom_call_target="tpu_custom_call" | custom-call | flops 21474836480 | bytes 10485760 | tf_op jit(solution)/shard_map/pallas_call | solution.py:165
  394.4 2.3 collective-permute-start.10
  399.6 2.6 convolution_convert_fusion.3
  402.5 9.6 %collective-permute-done.9 = bf16[512,768]{1,0:T(8,128)(2,1)} collective-permute-done((bf16[512,768]{1,0:T(8,128)(2,1)}, bf16[512,768]{1,0:T(8,128)(2,1)}, u32[]{:S(2)}, u32[]{:S(2)}) %collective-permute-start.9) | collective-permute-done | bytes 786464 | tf_op jit(solution)/shard_map/ppermute | solution.py:207
  413.8 50.7 %collective-permute-done.10 = bf16[512,768]{1,0:T(8,128)(2,1)} collective-permute-done((bf16[512,768]{1,0:T(8,128)(2,1)}, bf16[512,768]{1,0:T(8,128)(2,1)}, u32[]{:S(2)}, u32[]{:S(2)}) %collective-permute-start.10) | collective-permute-done | bytes 786464 | tf_op jit(solution)/shard_map/ppermute | solution.py:207
  472.7 2.1 slice_dynamic-update-slice_fusion.13
  485.9 2.8 dynamic-slice_convert_fusion.1
  488.7 3.0 copy.41
  493.6 2.6 maximum_multiply_fusion.2
  498.1 2.9 copy.45
  502.9 3.6 add_convert_fusion.1
  507.9 6.0 convolution_convert_fusion.1
  514.0 2.3 copy.48
  516.6 8.3 %fusion.23 = bf16[1,512,1024]{2,1,0:T(8,128)(2,1)} fusion(f32[512,1024]{1,0:T(8,128)S(1)} %copy-done.9, bf16[512,2624]{1,0:T(8,128)(2,1)} %copy-done.28, bf16[2624,1024]{1,0:T(8,128)(2,1)} %all-gather.11.cloned.1.call-done), kind=kOutput, calls=%fused_computation.56 | convolution fusion | flops 2752512000 | bytes 11206656 | tf_op jit(solution)/shard_map/dot_general | solution.py:270
  525.0 8.4 %fusion.21 = (f32[1024]{0:T(1024)S(1)}, f32[512]{0:T(512)S(1)}, f32[512]{0:T(512)S(1)}, f32[512,1024]{1,0:T(8,128)}) fusion(bf16[1,512,1024]{2,1,0:T(8,128)(2,1)S(1)} %copy-done.6, f32[512]{0:T(512)S(1)} %add_rsqrt_fusion.1, f32[512]{0:T(512)S(1)} %broadcast_multiply_fusion.6, f32[1024]{0:T(1024)S(1)} %bitcast.92, ...), kind=kOutput, calls=%fused_computation.34 | convolution fusion | flops 3235379200 | bytes 12599296 | tf_op jit(solution)/shard_map/re,de->rd/dot_general | solution.py:321
  533.4 37.9 %psum.39 = f32[2,1024]{1,0:T(2,128)S(1)} all-reduce(f32[2,1024]{1,0:T(2,128)S(1)} %pad_maximum_fusion.15), channel_id=1, replica_groups=mesh['fsdp'=8,'ctx'=4] {'fsdp','ctx'}, use_global_device_ids=true, to_apply=%region_18.0 | all-reduce | flops 2048 | bytes 16384 | tf_op jit(solution)/shard_map/psum | solution.py:339
  571.3 2.8 reduce-scatter.9.cloned.1.call-done
  574.1 86.8 %all-reduce.7.cloned.1.call-done = (bf16[128,5248]{1,0:T(8,128)(2,1)}, bf16[2624,128]{1,0:T(8,128)(2,1)}) async-done(((bf16[128,5248]{1,0:T(8,128)(2,1)}, bf16[2624,128]{1,0:T(8,128)(2,1)}), (bf16[128,5248]{1,0:T(8,128)(2,1)}, bf16[2624,128]{1,0:T(8,128)(2,1)})) %all-reduce.7.cloned.1.call-update) | async-done | bytes 2015248 | tf_op jit(solution)/shard_map/psum | solution.py:302
  661.4 3.7 fusion.20
  668.6 45.8 %all-reduce.5.cloned.1.call-done = (bf16[128,3072]{1,0:T(8,128)(2,1)}, bf16[128,1024]{1,0:T(8,128)(2,1)}) async-done(((bf16[128,3072]{1,0:T(8,128)(2,1)}, bf16[128,1024]{1,0:T(8,128)(2,1)}), (bf16[128,3072]{1,0:T(8,128)(2,1)}, bf16[128,1024]{1,0:T(8,128)(2,1)})) %all-reduce.5.cloned.1.call-update) | async-done | bytes 1048592 | tf_op jit(solution)/shard_map/psum | solution.py:335
  716.2 2.4 convert_element_type.126
  (167 shorter events, 78.5 us)
Async XLA Ops:
  7.2 2.9 copy-start.5
  7.2 51.0 %all-gather.5.cloned.1.call-start = ((), (), s32[]{:S(2)}) async-start(), calls=%async_computation.4 | async-start | bytes 7077888 | tf_op jit(solution)/shard_map/all_gather | solution.py:235
  7.9 239.6 %all-gather.7.cloned.1.call-start = ((), (), s32[]{:S(2)}) async-start(), calls=%async_computation.5 | async-start | bytes 2359296 | tf_op jit(solution)/shard_map/all_gather | solution.py:236
  8.7 2.1 copy-start.26
  8.7 2.1 copy-start.27
  8.7 242.4 %all-gather.9.cloned.1.call-start = ((), (), s32[]{:S(2)}) async-start(), calls=%async_computation.6 | async-start | bytes 12091392 | tf_op jit(solution)/shard_map/all_gather | solution.py:237
  9.4 254.9 %all-gather.11.cloned.1.call-start = ((), (), s32[]{:S(2)}) async-start(), calls=%async_computation.7 | async-start | bytes 6045696 | tf_op jit(solution)/shard_map/all_gather | solution.py:238
  10.0 504.0 %reduce-scatter.13.cloned.1.call-start = ((), (), s32[]{:S(2)}) async-start(), calls=%async_computation.11 | async-start | bytes 6193152
  24.8 68.4 %copy-start.2 = (f32[512,1024]{1,0:T(8,128)}, f32[512,1024]{1,0:T(8,128)S(1)}, u32[]{:S(2)}) copy-start(f32[512,1024]{1,0:T(8,128)S(1)} %copy.32) | copy-start | bytes 6291460
  63.9 2.7 copy-start.4
  91.8 1.9 copy-start.10
  97.2 22.4 %collective-permute-start = (bf16[512,768]{1,0:T(8,128)(2,1)S(1)}, bf16[512,768]{1,0:T(8,128)(2,1)S(1)}, u32[]{:S(2)}, u32[]{:S(2)}) collective-permute-start(bf16[512,768]{1,0:T(8,128)(2,1)S(1)} %pad_maximum_fusion.8), channel_id=1, source_target_pairs={{0,1},{1,2},{2,3},{3,0},{4,5},{5,6},{6,7},{7,4},{8,9},{9,10},{10,1... | collective-permute-start | bytes 2359304 | tf_op jit(solution)/shard_map/ppermute | solution.py:193
  98.8 53.7 %collective-permute-start.1 = (bf16[512,768]{1,0:T(8,128)(2,1)S(1)}, bf16[512,768]{1,0:T(8,128)(2,1)S(1)}, u32[]{:S(2)}, u32[]{:S(2)}) collective-permute-start(bf16[512,768]{1,0:T(8,128)(2,1)S(1)} %pad_maximum_fusion.9), channel_id=1, source_target_pairs={{0,2},{1,3},{2,0},{3,1},{4,6},{5,7},{6,4},{7,5},{8,10},{9,11},{10,... | collective-permute-start | bytes 2359304 | tf_op jit(solution)/shard_map/ppermute | solution.py:193
  101.3 51.2 %collective-permute-start.2 = (bf16[512,768]{1,0:T(8,128)(2,1)S(1)}, bf16[512,768]{1,0:T(8,128)(2,1)S(1)}, u32[]{:S(2)}, u32[]{:S(2)}) collective-permute-start(bf16[512,768]{1,0:T(8,128)(2,1)S(1)} %pad_maximum_fusion.10), channel_id=1, source_target_pairs={{0,3},{1,0},{2,1},{3,2},{4,7},{5,4},{6,5},{7,6},{8,11},{9,8},{10,9... | collective-permute-start | bytes 2359304 | tf_op jit(solution)/shard_map/ppermute | solution.py:193
  155.9 43.5 %copy-start = (bf16[2048,768]{1,0:T(8,128)(2,1)}, bf16[2048,768]{1,0:T(8,128)(2,1)S(1)}, u32[]{:S(2)}) copy-start(bf16[2048,768]{1,0:T(8,128)(2,1)S(1)} %pad_maximum_fusion.3.q_ref.k_ref.v_ref) | copy-start | bytes 9437188
  199.4 1.6 copy-start.1
  201.0 25.4 %collective-permute-start.3 = (bf16[512,256]{1,0:T(8,128)(2,1)}, bf16[512,256]{1,0:T(8,128)(2,1)S(1)}, u32[]{:S(2)}, u32[]{:S(2)}) collective-permute-start(bf16[512,256]{1,0:T(8,128)(2,1)} %get-tuple-element.72), channel_id=1, source_target_pairs={{0,3},{1,0},{2,1},{3,2},{4,7},{5,4},{6,5},{7,6},{8,11},{9,8},{10,9... | collective-permute-start | bytes 786440 | tf_op jit(solution)/shard_map/ppermute | solution.py:207
  219.2 23.9 %collective-permute-start.4 = (bf16[512,256]{1,0:T(8,128)(2,1)}, bf16[512,256]{1,0:T(8,128)(2,1)S(1)}, u32[]{:S(2)}, u32[]{:S(2)}) collective-permute-start(bf16[512,256]{1,0:T(8,128)(2,1)} %get-tuple-element.71), channel_id=1, source_target_pairs={{0,2},{1,3},{2,0},{3,1},{4,6},{5,7},{6,4},{7,5},{8,10},{9,11},{10,... | collective-permute-start | bytes 786440 | tf_op jit(solution)/shard_map/ppermute | solution.py:207
  219.8 24.1 %collective-permute-start.5 = (bf16[512,256]{1,0:T(8,128)(2,1)S(1)}, bf16[512,256]{1,0:T(8,128)(2,1)S(1)}, u32[]{:S(2)}, u32[]{:S(2)}) collective-permute-start(bf16[512,256]{1,0:T(8,128)(2,1)S(1)} %get-tuple-element.69), channel_id=1, source_target_pairs={{0,1},{1,2},{2,3},{3,0},{4,5},{5,6},{6,7},{7,4},{8,9},{9,10},{10,1... | collective-permute-start | bytes 786440 | tf_op jit(solution)/shard_map/ppermute | solution.py:207
  250.7 64.5 %copy-start.8 = (f32[512,1024]{1,0:T(8,128)}, f32[512,1024]{1,0:T(8,128)S(1)}, u32[]{:S(2)}) copy-start(f32[512,1024]{1,0:T(8,128)S(1)} %get-tuple-element.110) | copy-start | bytes 6291460
  251.1 13.2 %copy-start.18 = (bf16[1,512,1024]{2,1,0:T(8,128)(2,1)S(1)}, bf16[1,512,1024]{2,1,0:T(8,128)(2,1)}, u32[]{:S(2)}) copy-start(bf16[1,512,1024]{2,1,0:T(8,128)(2,1)} %param.15) | copy-start | bytes 3145732
  277.0 1.6 copy-start.28
  291.4 224.9 %reduce-scatter.7.cloned.1.call-start = ((), (), s32[]{:S(2)}) async-start(), calls=%async_computation.8 | async-start | bytes 12091392 | tf_op jit(solution)/shard_map/reduce_scatter | solution.py:296
  303.2 268.1 %reduce-scatter.11.cloned.1.call-start = ((), (), s32[]{:S(2)}) async-start(), calls=%async_computation.10 | async-start | bytes 2359296 | tf_op jit(solution)/shard_map/reduce_scatter | solution.py:329
  315.2 1.6 copy-start.25
  316.8 82.8 %copy-start.11 = (f32[512,1024]{1,0:T(8,128)}, f32[512,1024]{1,0:T(8,128)S(1)}, u32[]{:S(2)}) copy-start(f32[512,1024]{1,0:T(8,128)S(1)} %multiply_add_fusion) | copy-start | bytes 6291460
  318.3 8.7 %collective-permute-start.8 = (bf16[512,256]{1,0:T(8,128)(2,1)S(1)}, bf16[512,256]{1,0:T(8,128)(2,1)S(1)}, u32[]{:S(2)}, u32[]{:S(2)}) collective-permute-start(bf16[512,256]{1,0:T(8,128)(2,1)S(1)} %get-tuple-element.66), channel_id=1, source_target_pairs={{0,3},{1,0},{2,1},{3,2},{4,7},{5,4},{6,5},{7,6},{8,11},{9,8},{10,9... | collective-permute-start | bytes 786440 | tf_op jit(solution)/shard_map/ppermute | solution.py:193
  318.3 23.5 %collective-permute-start.7 = (bf16[512,256]{1,0:T(8,128)(2,1)S(1)}, bf16[512,256]{1,0:T(8,128)(2,1)S(1)}, u32[]{:S(2)}, u32[]{:S(2)}) collective-permute-start(bf16[512,256]{1,0:T(8,128)(2,1)S(1)} %get-tuple-element.67), channel_id=1, source_target_pairs={{0,2},{1,3},{2,0},{3,1},{4,6},{5,7},{6,4},{7,5},{8,10},{9,11},{10,... | collective-permute-start | bytes 786440 | tf_op jit(solution)/shard_map/ppermute | solution.py:193
  319.0 22.8 %collective-permute-start.6 = (bf16[512,256]{1,0:T(8,128)(2,1)S(1)}, bf16[512,256]{1,0:T(8,128)(2,1)S(1)}, u32[]{:S(2)}, u32[]{:S(2)}) collective-permute-start(bf16[512,256]{1,0:T(8,128)(2,1)S(1)} %get-tuple-element.68), channel_id=1, source_target_pairs={{0,1},{1,2},{2,3},{3,0},{4,5},{5,6},{6,7},{7,4},{8,9},{9,10},{10,1... | collective-permute-start | bytes 786440 | tf_op jit(solution)/shard_map/ppermute | solution.py:193
  392.5 7.1 copy-start.24
  393.4 18.7 %collective-permute-start.9 = (bf16[512,768]{1,0:T(8,128)(2,1)}, bf16[512,768]{1,0:T(8,128)(2,1)}, u32[]{:S(2)}, u32[]{:S(2)}) collective-permute-start(bf16[512,768]{1,0:T(8,128)(2,1)} %pad_maximum_fusion.11), channel_id=1, source_target_pairs={{0,3},{1,0},{2,1},{3,2},{4,7},{5,4},{6,5},{7,6},{8,11},{9,8},{10,9... | collective-permute-start | bytes 2359304 | tf_op jit(solution)/shard_map/ppermute | solution.py:207
  394.4 70.1 %collective-permute-start.10 = (bf16[512,768]{1,0:T(8,128)(2,1)}, bf16[512,768]{1,0:T(8,128)(2,1)}, u32[]{:S(2)}, u32[]{:S(2)}) collective-permute-start(bf16[512,768]{1,0:T(8,128)(2,1)} %pad_maximum_fusion.12), channel_id=1, source_target_pairs={{0,2},{1,3},{2,0},{3,1},{4,6},{5,7},{6,4},{7,5},{8,10},{9,11},{10,... | collective-permute-start | bytes 2359304 | tf_op jit(solution)/shard_map/ppermute | solution.py:207
  397.6 68.6 %collective-permute-start.11 = (bf16[512,768]{1,0:T(8,128)(2,1)}, bf16[512,768]{1,0:T(8,128)(2,1)}, u32[]{:S(2)}, u32[]{:S(2)}) collective-permute-start(bf16[512,768]{1,0:T(8,128)(2,1)} %pad_maximum_fusion.13), channel_id=1, source_target_pairs={{0,1},{1,2},{2,3},{3,0},{4,5},{5,6},{6,7},{7,4},{8,9},{9,10},{10,1... | collective-permute-start | bytes 2359304 | tf_op jit(solution)/shard_map/ppermute | solution.py:207
  402.3 171.8 %reduce-scatter.9.cloned.1.call-start = ((), (), s32[]{:S(2)}) async-start(), calls=%async_computation.9 | async-start | bytes 7077888 | tf_op jit(solution)/shard_map/reduce_scatter | solution.py:326
  402.5 66.2 %copy-start.13 = (bf16[512,2048]{1,0:T(8,128)(2,1)S(1)}, bf16[512,2048]{1,0:T(8,128)(2,1)}, u32[]{:S(2)}) copy-start(bf16[512,2048]{1,0:T(8,128)(2,1)} %get-tuple-element.57) | copy-start | bytes 6291460
  491.7 1.6 copy-start.7
  501.0 1.9 copy-start.3
  502.9 3.6 copy-start.16
  502.9 4.9 copy-start.6
  513.9 2.7 copy-start.9
  513.9 147.0 %all-reduce.7.cloned.1.call-start = ((), (), s32[]{:S(2)}) async-start(), calls=%async_computation.13 | async-start | bytes 4030464 | tf_op jit(solution)/shard_map/psum | solution.py:302
  516.3 198.1 %all-reduce.5.cloned.1.call-start = ((), (), s32[]{:S(2)}) async-start(), calls=%async_computation.12 | async-start | bytes 2097152 | tf_op jit(solution)/shard_map/psum | solution.py:335
  516.6 8.4 %copy-start.17 = (bf16[512,1024]{1,0:T(8,128)(2,1)S(1)}, bf16[512,1024]{1,0:T(8,128)(2,1)}, u32[]{:S(2)}) copy-start(bf16[512,1024]{1,0:T(8,128)(2,1)} %copy-done.16) | copy-start | bytes 3145732
  516.6 8.4 %copy-start.20 = (bf16[512,1024]{1,0:T(8,128)(2,1)S(1)}, bf16[512,1024]{1,0:T(8,128)(2,1)}, u32[]{:S(2)}) copy-start(bf16[512,1024]{1,0:T(8,128)(2,1)} %copy-done.19) | copy-start | bytes 3145732
  516.6 8.4 %copy-start.22 = (bf16[512,1024]{1,0:T(8,128)(2,1)S(1)}, bf16[512,1024]{1,0:T(8,128)(2,1)}, u32[]{:S(2)}) copy-start(bf16[512,1024]{1,0:T(8,128)(2,1)} %copy-done.21) | copy-start | bytes 3145732
  525.0 136.4 %copy-start.12 = (f32[512,1024]{1,0:T(8,128)S(1)}, f32[512,1024]{1,0:T(8,128)}, u32[]{:S(2)}) copy-start(f32[512,1024]{1,0:T(8,128)} %copy-done.11) | copy-start | bytes 6291460
  661.4 3.7 copy-start.23
  665.1 1.8 copy-start.15
  (3 other events, 3.7 us)
Sparse Core Ops, SparseCore 0:
  9.9 48.2 all-gather.4
  60.0 27.8 all-gather.6
  89.9 64.3 all-gather.8
  156.0 42.6 all-gather.10
  291.5 55.0 reduce-scatter.12
  350.4 82.8 reduce-scatter.6
  436.5 41.1 reduce-scatter.10
  514.0 60.0 reduce-scatter.8
  576.6 84.2 all-reduce.6
  663.3 51.1 all-reduce.4

commit v2 on v1

--- a/solution.py
+++ b/solution.py
@@ -180,12 +180,18 @@
     )(*thirds(packed), attended, log_total, grad)
 
 
-def to_heads(arrays):
+def group_count(model_width):
+    share = model_width // lax.axis_size("ctx")
+    return share // 128 if share % 128 == 0 else 1
+
+
+def to_heads(arrays, group, groups):
     count, me = lax.axis_size("ctx"), lax.axis_index("ctx")
-    width = arrays[0].shape[1] // count
+    share = arrays[0].shape[1] // count
+    width = share // groups
     received = []
     for step in range(count):
-        start = lax.rem(me + step, count) * width
+        start = lax.rem(me + step, count) * share + group * width
         piece = jnp.concatenate(
             [lax.dynamic_slice_in_dim(item, start, width, 1) for item in arrays], 1
         )
@@ -214,6 +220,22 @@
         turned = [item[:, number * width : (number + 1) * width] for item in received]
         doubled = jnp.concatenate(turned + turned, 1)
         results.append(lax.dynamic_slice_in_dim(doubled, start, count * width, 1))
+    return results
+
+
+def join(groups):
+    count = lax.axis_size("ctx")
+    if len(groups) == 1:
+        return groups[0]
+    results = []
+    for parts in zip(*groups):
+        width = parts[0].shape[1] // count
+        pieces = [
+            part[:, owner * width : (owner + 1) * width]
+            for owner in range(count)
+            for part in parts
+        ]
+        results.append(jnp.concatenate(pieces, 1))
     return results
 
 
@@ -251,9 +273,10 @@
     ).astype(jnp.bfloat16)
     keys = keys.reshape(local_rows, model_width)
     values = query_key_value[:, 2 * model_width :].astype(jnp.bfloat16)
-    packed = to_heads((query, keys, values))
-    attended, log_total = attend(packed)
-    (attn_low,) = to_rows((attended.astype(jnp.bfloat16),))
+    groups = group_count(model_width)
+    packed = [to_heads((query, keys, values), group, groups) for group in range(groups)]
+    forward = [attend(item) for item in packed]
+    (attn_low,) = join([to_rows((item[0].astype(jnp.bfloat16),)) for item in forward])
     middle_activation = inputs + jnp.dot(attn_low, full_attn, preferred_element_type=jnp.float32)
     normed_two, inv_two = normalize(middle_activation)
     hidden_after_feedforward = (normed_two * full_two.astype(jnp.float32)).astype(jnp.bfloat16)
@@ -299,12 +322,22 @@
     part_wout = lax.psum_scatter(
         grad_wout.astype(jnp.bfloat16), "fsdp", scatter_dimension=1, tiled=True
     )
-    sum_win, sum_wout = lax.psum((part_win, part_wout), "ctx")
     grad_branch = grad_middle.astype(jnp.bfloat16)
     grad_wattn = jnp.einsum("rd,re->de", attn_low, grad_branch, preferred_element_type=jnp.float32)
+    part_wattn = lax.psum_scatter(
+        grad_wattn.astype(jnp.bfloat16), "fsdp", scatter_dimension=0, tiled=True
+    )
+    sum_win, sum_wout, sum_wattn = lax.psum((part_win, part_wout, part_wattn), "ctx")
     grad_attn = jnp.einsum("re,de->rd", grad_branch, back_attn, preferred_element_type=jnp.float32)
-    (grad_heads,) = (to_heads((grad_attn.astype(jnp.bfloat16),)),)
-    back_query, back_keys, grad_v = to_rows(attend_back(packed, attended, log_total, grad_heads))
+    grad_attn = grad_attn.astype(jnp.bfloat16)
+    back_query, back_keys, grad_v = join(
+        [
+            to_rows(
+                attend_back(packed[group], *forward[group], to_heads((grad_attn,), group, groups))
+            )
+            for group in range(groups)
+        ]
+    )
     grad_q = rotate(back_query.reshape(head_shape).astype(jnp.float32), cosine, -sine)
     grad_k = rotate(back_keys.reshape(head_shape).astype(jnp.float32), cosine, -sine)
     grad_qkv_rows = jnp.concatenate(
@@ -323,16 +356,11 @@
     grad_inputs = grad_middle + norm_back(
         grad_hone * back_one.astype(jnp.float32), normed_one, inv_one
     )
-    part_wqkv = lax.psum_scatter(
-        grad_wqkv.astype(jnp.bfloat16), "fsdp", scatter_dimension=0, tiled=True
-    )
-    part_wattn = lax.psum_scatter(
-        grad_wattn.astype(jnp.bfloat16), "fsdp", scatter_dimension=0, tiled=True
-    )
-    sum_win, sum_wout, part_wqkv, part_wattn = lax.optimization_barrier(
-        (sum_win, sum_wout, part_wqkv, part_wattn)
-    )
-    sum_wqkv, sum_wattn = lax.psum((part_wqkv, part_wattn), "ctx")
+    sum_win, sum_wout, sum_wattn, grad_wqkv = lax.optimization_barrier(
+        (sum_win, sum_wout, sum_wattn, grad_wqkv.astype(jnp.bfloat16))
+    )
+    part_wqkv = lax.psum_scatter(grad_wqkv, "fsdp", scatter_dimension=0, tiled=True)
+    sum_wqkv = lax.psum(part_wqkv, "ctx")
     sum_win, sum_wout, sum_wqkv, sum_wattn = (
         item.astype(jnp.float32) for item in (sum_win, sum_wout, sum_wqkv, sum_wattn)
     )

time: 733 us -> 686 us (0.936)
  waiting for transfers between devices: 324 us -> 261 us
  starting transfers between devices: 33 us -> 56.3 us
    ppermute x6 -> x12, waiting for transfers between devices: 82.6 us -> 49.4 us  [to_rows(): lax.ppermute(piece, 'ctx', [(source, (source - step) % count) for source...]
    ppermute x6 -> x12, waiting for transfers between devices: 70.3 us -> 37.5 us  [to_heads(): lax.ppermute(piece, 'ctx', [(source, (source + step) % count) for source...]
    ppermute x6 -> x12, starting transfers between devices: 8.46 us -> 21.6 us  [to_heads(): lax.ppermute(piece, 'ctx', [(source, (source + step) % count) for source...]
    ppermute x6 -> x12, starting transfers between devices: 23.3 us -> 33.9 us  [to_rows(): lax.ppermute(piece, 'ctx', [(source, (source - step) % count) for source...]
    psum x2, waiting for transfers between devices: 133 us -> 123 us  [the longest x1 84.6 us: local(): lax.psum((part_win, part_wout, part_wattn), 'ctx')]
    convert_element_type x4 -> x2, other arithmetic: 8.06 us -> 0.11 us  [local(): item[0].astype(jnp.bfloat16)]
    reduce_scatter x1, waiting for transfers between devices: 0.01 us -> 7.65 us  [local(): lax.psum_scatter(grad_win.astype(jnp.bfloat16), 'fsdp', scatter_dimension...]
    pallas_call x1 -> x2, Pallas kernels: 48.2 us -> 46 us  [attend_back(): pl.pallas_call(attend_back_kernel, grid=grid, in_specs=column + [by_rows,...]
  transfers between devices with their start and end apart: 22 -> 34, of which waited for: 12 -> 16; matrix products, arithmetic and copies ran while one was open for 24% -> 24% of each run, Pallas kernels for 13% -> 13%
where the time goes in v2:
time: 686 us; the launch traced here: 679 us
  waiting for transfers between devices  261 us (38%)
  matrix products  94.6 us (14%)
  Pallas kernels  89.1 us (13%)
  local copies, waits for them, and re-layouts  73.7 us (11%)
  starting transfers between devices  56.3 us (8%)
  blocking collectives  49.3 us (7%)
  other arithmetic  39.4 us (6%)
  between operations  15.6 us (2%)
    psum x1, waiting for transfers between devices, local(): lax.psum((part_win, part_wout, part_wattn), 'ctx')  84.6 us
    ppermute x12, waiting for transfers between devices, to_rows(): lax.ppermute(piece, 'ctx', [(source, (source - step) % count) for source...  49.4 us
    pallas_call x2, Pallas kernels, attend_back(): pl.pallas_call(attend_back_kernel, grid=grid, in_specs=column + [by_rows,...  46 us
    unnamed x146, local copies, waits for them, and re-layouts  43.2 us
    pallas_call x2, Pallas kernels, attend(): pl.pallas_call(attend_kernel, grid=grid, in_specs=column, out_specs=(by_r...  43.1 us
    psum x1, blocking collectives, local(): gains = lax.psum(jnp.stack([grad_one, grad_two]), ('fsdp', 'ctx'))  39.1 us
    psum x1, waiting for transfers between devices, local(): sum_wqkv = lax.psum(part_wqkv, 'ctx')  37.9 us
    ppermute x12, waiting for transfers between devices, to_heads(): lax.ppermute(piece, 'ctx', [(source, (source + step) % count) for source...  37.5 us
  transfers between devices with their start and end apart: 34, of which 16 were waited for; matrix products, arithmetic and copies ran while one was open for 24% of the time, Pallas kernels for 13%

profile of v2, /device:TPU:0, one launch (start us, length us, event | category | flops | bytes accessed | tf_op | source)
XLA Modules:
  0.0 678.8 jit_solution(2421598773488496219)
XLA Ops:
  10.8 10.2 %all_gather.15 = bf16[2,1024]{1,0:T(2,128)(2,1)S(1)} all-gather(bf16[2,128]{1,0:T(2,128)(2,1)S(1)} %pad_maximum_fusion.21), channel_id=1, replica_groups=mesh['fsdp'=8,'ctx'=4] {'fsdp'}, dimensions={1}, use_global_device_ids=true | all-gather | bytes 4608 | tf_op jit(solution)/shard_map/all_gather | solution.py:261
  24.9 33.2 %all-gather.5.cloned.1.call-done = bf16[1024,3072]{1,0:T(8,128)(2,1)} async-done(((bf16[128,3072]{1,0:T(8,128)(2,1)}), bf16[1024,3072]{1,0:T(8,128)(2,1)}) %all-gather.5.cloned.1.call-update) | async-done | bytes 6291472 | tf_op jit(solution)/shard_map/all_gather | solution.py:257
  58.2 5.7 fusion.38
  63.9 2.6 copy-done.6
  68.0 2.9 copy.36
  74.2 2.9 copy.37
  77.1 5.2 fusion.41
  82.3 2.9 copy.33
  88.5 2.9 copy.34
  93.2 3.1 fusion.24
  106.0 5.5 collective-permute-done.6
  113.8 14.6 %collective-permute-done.7 = bf16[512,384]{1,0:T(8,128)(2,1)S(1)} collective-permute-done((bf16[512,384]{1,0:T(8,128)(2,1)}, bf16[512,384]{1,0:T(8,128)(2,1)S(1)}, u32[]{:S(2)}, u32[]{:S(2)}) %collective-permute-start.7) | collective-permute-done | bytes 393248 | tf_op jit(solution)/shard_map/ppermute | solution.py:199
  130.7 21.6 %shard_map.144 = (f32[2048,128]{1,0:T(8,128)S(1)}, f32[1,2,2048]{2,1,0:T(2,128)S(1)}) custom-call(bf16[2048,384]{1,0:T(8,128)(2,1)S(1)} %pad_maximum_fusion.4.q_ref.k_ref.v_ref, bf16[2048,384]{1,0:T(8,128)(2,1)S(1)} %pad_maximum_fusion.4.q_ref.k_ref.v_ref, bf16[2048,384]{1,0:T(8,128)(2,1)S(1)} %pad_maximum_fusion.4.q_ref.k_ref.v_ref), custom_call_target="tpu_custom_call" | custom-call | flops 4294967296 | bytes 2621440 | tf_op jit(solution)/shard_map/pallas_call | solution.py:144
  152.4 9.1 %collective-permute-done.1 = bf16[512,384]{1,0:T(8,128)(2,1)S(1)} collective-permute-done((bf16[512,384]{1,0:T(8,128)(2,1)S(1)}, bf16[512,384]{1,0:T(8,128)(2,1)S(1)}, u32[]{:S(2)}, u32[]{:S(2)}) %collective-permute-start.1) | collective-permute-done | bytes 393248 | tf_op jit(solution)/shard_map/ppermute | solution.py:199
  161.6 21.6 %shard_map.143 = (f32[2048,128]{1,0:T(8,128)S(1)}, f32[1,2,2048]{2,1,0:T(2,128)S(1)}) custom-call(bf16[2048,384]{1,0:T(8,128)(2,1)S(1)} %pad_maximum_fusion.3.q_ref.k_ref.v_ref, bf16[2048,384]{1,0:T(8,128)(2,1)S(1)} %pad_maximum_fusion.3.q_ref.k_ref.v_ref, bf16[2048,384]{1,0:T(8,128)(2,1)S(1)} %pad_maximum_fusion.3.q_ref.k_ref.v_ref), custom_call_target="tpu_custom_call" | custom-call | flops 4294967296 | bytes 2621440 | tf_op jit(solution)/shard_map/pallas_call | solution.py:144
  183.3 16.7 %collective-permute-start.5 = (bf16[512,128]{1,0:T(8,128)(2,1)S(1)}, bf16[512,128]{1,0:T(8,128)(2,1)S(1)}, u32[]{:S(2)}, u32[]{:S(2)}) collective-permute-start(bf16[512,128]{1,0:T(8,128)(2,1)S(1)} %get-tuple-element.120), channel_id=1, source_target_pairs={{0,1},{1,2},{2,3},{3,0},{4,5},{5,6},{6,7},{7,4},{8,9},{9,10},{10,1... | collective-permute-start | bytes 393224 | tf_op jit(solution)/shard_map/ppermute | solution.py:213
  205.1 4.5 collective-permute-done.3
  209.5 4.5 collective-permute-start.9
  216.8 7.3 %collective-permute-done.9 = bf16[512,128]{1,0:T(8,128)(2,1)S(1)} collective-permute-done((bf16[512,128]{1,0:T(8,128)(2,1)S(1)}, bf16[512,128]{1,0:T(8,128)(2,1)S(1)}, u32[]{:S(2)}, u32[]{:S(2)}) %collective-permute-start.9) | collective-permute-done | bytes 131104 | tf_op jit(solution)/shard_map/ppermute | solution.py:213
  229.3 3.5 fusion.46
  234.5 13.0 %fusion.40 = f32[512,5248]{1,0:T(8,128)} fusion(bf16[1024,5248]{1,0:T(8,128)(2,1)} %all-gather.9.cloned.1.call-done, f32[512,1024]{1,0:T(8,128)} %copy-done.11, f32[1024]{0:T(1024)S(1)} %bitcast.98, f32[512]{0:T(512)S(1)} %add_rsqrt_fusion, f32[512]{0:T(512)S(1)} %broadcast_multiply_fusion.5), kind=kOutput, calls=%fused_computation.236 | convolution fusion | flops 5505024000 | bytes 23601152 | tf_op jit(solution)/shard_map/dot_general | solution.py:283
  247.5 12.3 %fusion.5 = (bf16[512,2624]{1,0:T(8,128)(2,1)}, bf16[512,2624]{1,0:T(8,128)(2,1)}, bf16[512,2624]{1,0:T(8,128)(2,1)S(1)}) fusion(f32[512,5248]{1,0:T(8,128)} %fusion.40, bf16[2624,1024]{1,0:T(8,128)(2,1)} %all-gather.11.cloned.1.call-done, bf16[1,512,1024]{2,1,0:T(8,128)(2,1)} %param.15), kind=kOutput, calls=%fused_computation.9 | convolution fusion | flops 2772959232 | bytes 25231360 | tf_op jit(solution)/shard_map/rd,fd->rf/dot_general | solution.py:307
  261.3 4.8 convolution_convert_fusion.2
  266.1 8.0 %copy.47 = bf16[2624,1024]{0,1:T(8,128)(2,1)} copy(bf16[2624,1024]{1,0:T(8,128)(2,1)} %convolution_convert_fusion.2) | data formatting | bytes 10747904
  274.4 13.2 %multiply_reduce_fusion = (f32[1024]{0:T(1024)S(1)}, f32[512]{0:T(512)S(1)}, f32[512]{0:T(512)S(1)}, f32[512,1024]{1,0:T(8,128)}) fusion(f32[512,1024]{1,0:T(8,128)} %copy-done.11, f32[512]{0:T(512)S(1)} %add_rsqrt_fusion, f32[512]{0:T(512)S(1)} %broadcast_multiply_fusion.5, f32[1024]{0:T(1024)S(1)} %bitcast.99, ...), kind=kOutput, calls=%fused_computation.39 | convolution fusion | flops 5517867008 | bytes 20332544 | tf_op jit(solution)/shard_map/rf,df->rd/dot_general | solution.py:314
  287.6 2.6 multiply_add_fusion
  291.5 3.9 convolution_convert_fusion.3
  295.5 12.4 %convolution_convert_fusion = bf16[1024,5248]{1,0:T(8,128)(2,1)} fusion(bf16[512,2624]{1,0:T(8,128)(2,1)} %get-tuple-element.46, bf16[512,2624]{1,0:T(8,128)(2,1)} %get-tuple-element.45, f32[512,1024]{1,0:T(8,128)} %copy-done.11, f32[1024]{0:T(1024)S(1)} %bitcast.101, f32[512]{0:T(512)S(1)} %add_rsqrt_fusion, f32[512]{0:T(512)S(1)} %broadcast_multiply_fusion.5), kind=kOutput, calls=%fused_computation | convolution fusion | flops 5521145856 | bytes 18227200 | tf_op jit(solution)/shard_map/rd,rf->df/dot_general | solution.py:311
  308.0 3.5 convolution_convert_fusion.4
  314.4 3.8 collective-permute-start.20
  319.0 6.2 collective-permute-start.18
  325.2 7.6 %collective-permute-done.13 = bf16[512,128]{1,0:T(8,128)(2,1)S(1)} collective-permute-done((bf16[512,128]{1,0:T(8,128)(2,1)S(1)}, bf16[512,128]{1,0:T(8,128)(2,1)S(1)}, u32[]{:S(2)}, u32[]{:S(2)}) %collective-permute-start.13) | collective-permute-done | bytes 131104 | tf_op jit(solution)/shard_map/ppermute | solution.py:199
  332.9 23.0 %shard_map.145 = (bf16[2048,128]{1,0:T(8,128)(2,1)S(1)}, bf16[2048,128]{1,0:T(8,128)(2,1)S(1)}, bf16[2048,128]{1,0:T(8,128)(2,1)S(1)}) custom-call(bf16[2048,384]{1,0:T(8,128)(2,1)S(1)} %pad_maximum_fusion.3.q_ref.k_ref.v_ref, bf16[2048,384]{1,0:T(8,128)(2,1)S(1)} %pad_maximum_fusion.3.q_ref.k_ref.v_ref, ...), custom_call_target="tpu_custom_call" | custom-call | flops 10737418240 | bytes 5242880 | tf_op jit(solution)/shard_map/pallas_call | solution.py:165
  358.6 23.0 %shard_map.146 = (bf16[2048,128]{1,0:T(8,128)(2,1)S(1)}, bf16[2048,128]{1,0:T(8,128)(2,1)S(1)}, bf16[2048,128]{1,0:T(8,128)(2,1)S(1)}) custom-call(bf16[2048,384]{1,0:T(8,128)(2,1)S(1)} %pad_maximum_fusion.4.q_ref.k_ref.v_ref, bf16[2048,384]{1,0:T(8,128)(2,1)S(1)} %pad_maximum_fusion.4.q_ref.k_ref.v_ref, ...), custom_call_target="tpu_custom_call" | custom-call | flops 10737418240 | bytes 5242880 | tf_op jit(solution)/shard_map/pallas_call | solution.py:165
  387.5 6.9 %collective-permute-done.16 = bf16[512,384]{1,0:T(8,128)(2,1)S(1)} collective-permute-done((bf16[512,384]{1,0:T(8,128)(2,1)S(1)}, bf16[512,384]{1,0:T(8,128)(2,1)S(1)}, u32[]{:S(2)}, u32[]{:S(2)}) %collective-permute-start.16) | collective-permute-done | bytes 393248 | tf_op jit(solution)/shard_map/ppermute | solution.py:213
  395.5 5.8 collective-permute-done.21
  401.4 23.1 %collective-permute-done.22 = bf16[512,384]{1,0:T(8,128)(2,1)S(1)} collective-permute-done((bf16[512,384]{1,0:T(8,128)(2,1)S(1)}, bf16[512,384]{1,0:T(8,128)(2,1)S(1)}, u32[]{:S(2)}, u32[]{:S(2)}) %collective-permute-start.22) | collective-permute-done | bytes 393248 | tf_op jit(solution)/shard_map/ppermute | solution.py:213
  439.8 2.6 copy.44
  446.7 2.9 copy.45
  453.8 7.7 %reduce-scatter.7.cloned.1.call-done = bf16[128,5248]{1,0:T(8,128)(2,1)} async-done(((bf16[1024,5248]{1,0:T(8,128)(2,1)}), bf16[128,5248]{1,0:T(8,128)(2,1)}) %reduce-scatter.7.cloned.1.call-update) | async-done | bytes 1343504 | tf_op jit(solution)/shard_map/reduce_scatter | solution.py:319
  468.2 5.7 convolution_convert_fusion.1
  474.0 84.6 %all-reduce.6.cloned.1.call-done = (bf16[128,5248]{1,0:T(8,128)(2,1)}, bf16[2624,128]{1,0:T(8,128)(2,1)}, bf16[128,1024]{1,0:T(8,128)(2,1)}) async-done(((bf16[128,5248]{1,0:T(8,128)(2,1)}, bf16[2624,128]{1,0:T(8,128)(2,1)}, bf16[128,1024]{1,0:T(8,128)(2,1)}), (bf16[128,5248]{1,0:T(8,128)(2,1)}, bf16[2624,128]{1,0:T(8,128)(2,1)}, bf16[128,1024]{1,0:T(8,128)(2,1)})) %all-reduce.6.cloned.1.call-update) | async-done | bytes 2277392 | tf_op jit(solution)/shard_map/psum | solution.py:330
  560.2 7.6 %fusion.23 = bf16[1,512,1024]{2,1,0:T(8,128)(2,1)} fusion(f32[512,1024]{1,0:T(8,128)S(1)} %copy-done.13, bf16[512,2624]{1,0:T(8,128)(2,1)} %copy-done.39, bf16[2624,1024]{1,0:T(8,128)(2,1)} %all-gather.11.cloned.1.call-done), kind=kOutput, calls=%fused_computation.56 | convolution fusion | flops 2752512000 | bytes 11206656 | tf_op jit(solution)/shard_map/dot_general | solution.py:293
  567.8 9.0 %fusion.21 = (f32[1024]{0:T(1024)S(1)}, f32[512]{0:T(512)S(1)}, f32[512]{0:T(512)S(1)}, f32[512,1024]{1,0:T(8,128)}) fusion(bf16[1,512,1024]{2,1,0:T(8,128)(2,1)S(1)} %copy-done.8, f32[512]{0:T(512)S(1)} %add_rsqrt_fusion.1, f32[512]{0:T(512)S(1)} %broadcast_multiply_fusion.6, f32[1024]{0:T(1024)S(1)} %bitcast.96, bf16[512,3072]{1,0:T(8,128)(2,1)S(1)} %copy-done.35, ...), kind=kOutput, calls=%fused_computation.32 | convolution fusion | flops 3225942016 | bytes 12599296 | tf_op jit(solution)/shard_map/re,de->rd/dot_general | solution.py:354
  576.8 39.1 %psum.39 = f32[2,1024]{1,0:T(2,128)S(1)} all-reduce(f32[2,1024]{1,0:T(2,128)S(1)} %pad_maximum_fusion.20), channel_id=1, replica_groups=mesh['fsdp'=8,'ctx'=4] {'fsdp','ctx'}, use_global_device_ids=true, to_apply=%region_18.0 | all-reduce | flops 2048 | bytes 16384 | tf_op jit(solution)/shard_map/psum | solution.py:367
  615.9 7.6 %reduce-scatter.11.cloned.1.call-done = bf16[128,3072]{1,0:T(8,128)(2,1)} async-done(((bf16[1024,3072]{1,0:T(8,128)(2,1)}), bf16[128,3072]{1,0:T(8,128)(2,1)}) %reduce-scatter.11.cloned.1.call-update) | async-done | bytes 786448 | tf_op jit(solution)/shard_map/reduce_scatter | solution.py:362
  624.0 3.7 fusion.20
  631.4 37.9 %all-reduce.4.cloned.1.call-done = bf16[128,3072]{1,0:T(8,128)(2,1)} async-done(((bf16[128,3072]{1,0:T(8,128)(2,1)}), bf16[128,3072]{1,0:T(8,128)(2,1)}) %all-reduce.4.cloned.1.call-update) | async-done | bytes 786448 | tf_op jit(solution)/shard_map/psum | solution.py:363
  (277 shorter events, 101.3 us)
Async XLA Ops:
  7.2 51.0 %all-gather.5.cloned.1.call-start = ((), (), s32[]{:S(2)}) async-start(), calls=%async_computation.4 | async-start | bytes 7077888 | tf_op jit(solution)/shard_map/all_gather | solution.py:257
  7.9 221.4 %all-gather.7.cloned.1.call-start = ((), (), s32[]{:S(2)}) async-start(), calls=%async_computation.5 | async-start | bytes 2359296 | tf_op jit(solution)/shard_map/all_gather | solution.py:258
  8.7 225.8 %all-gather.9.cloned.1.call-start = ((), (), s32[]{:S(2)}) async-start(), calls=%async_computation.6 | async-start | bytes 12091392 | tf_op jit(solution)/shard_map/all_gather | solution.py:259
  9.4 238.1 %all-gather.11.cloned.1.call-start = ((), (), s32[]{:S(2)}) async-start(), calls=%async_computation.7 | async-start | bytes 6045696 | tf_op jit(solution)/shard_map/all_gather | solution.py:260
  10.0 441.5 %reduce-scatter.13.cloned.1.call-start = ((), (), s32[]{:S(2)}) async-start(), calls=%async_computation.12 | async-start | bytes 6193152
  24.9 67.5 %copy-start.4 = (f32[512,1024]{1,0:T(8,128)}, f32[512,1024]{1,0:T(8,128)S(1)}, u32[]{:S(2)}) copy-start(f32[512,1024]{1,0:T(8,128)S(1)} %copy.32) | copy-start | bytes 6291460
  97.5 7.8 %copy-start.23 = (bf16[512,128]{1,0:T(8,128)(2,1)S(1)}, bf16[512,128]{1,0:T(8,128)(2,1)}, u32[]{:S(2)}) copy-start(bf16[512,128]{1,0:T(8,128)(2,1)} %get-tuple-element.81) | copy-start | bytes 393220
  97.5 8.4 %copy-start.22 = (bf16[512,128]{1,0:T(8,128)(2,1)S(1)}, bf16[512,128]{1,0:T(8,128)(2,1)}, u32[]{:S(2)}) copy-start(bf16[512,128]{1,0:T(8,128)(2,1)} %get-tuple-element.80) | copy-start | bytes 393220
  97.6 13.9 %collective-permute-start.6 = (bf16[512,384]{1,0:T(8,128)(2,1)S(1)}, bf16[512,384]{1,0:T(8,128)(2,1)S(1)}, u32[]{:S(2)}, u32[]{:S(2)}) collective-permute-start(bf16[512,384]{1,0:T(8,128)(2,1)S(1)} %pad_maximum_fusion.10), channel_id=1, source_target_pairs={{0,1},{1,2},{2,3},{3,0},{4,5},{5,6},{6,7},{7,4},{8,9},{9,10},{10,1... | collective-permute-start | bytes 1179656 | tf_op jit(solution)/shard_map/ppermute | solution.py:199
  100.0 28.5 %collective-permute-start.7 = (bf16[512,384]{1,0:T(8,128)(2,1)}, bf16[512,384]{1,0:T(8,128)(2,1)S(1)}, u32[]{:S(2)}, u32[]{:S(2)}) collective-permute-start(bf16[512,384]{1,0:T(8,128)(2,1)} %pad_maximum_fusion.11), channel_id=1, source_target_pairs={{0,2},{1,3},{2,0},{3,1},{4,6},{5,7},{6,4},{7,5},{8,10},{9,11},{10,... | collective-permute-start | bytes 1179656 | tf_op jit(solution)/shard_map/ppermute | solution.py:199
  103.2 25.3 %collective-permute-start.8 = (bf16[512,384]{1,0:T(8,128)(2,1)}, bf16[512,384]{1,0:T(8,128)(2,1)S(1)}, u32[]{:S(2)}, u32[]{:S(2)}) collective-permute-start(bf16[512,384]{1,0:T(8,128)(2,1)} %pad_maximum_fusion.12), channel_id=1, source_target_pairs={{0,3},{1,0},{2,1},{3,2},{4,7},{5,4},{6,5},{7,6},{8,11},{9,8},{10,9... | collective-permute-start | bytes 1179656 | tf_op jit(solution)/shard_map/ppermute | solution.py:199
  104.7 47.7 %collective-permute-start = (bf16[512,384]{1,0:T(8,128)(2,1)S(1)}, bf16[512,384]{1,0:T(8,128)(2,1)S(1)}, u32[]{:S(2)}, u32[]{:S(2)}) collective-permute-start(bf16[512,384]{1,0:T(8,128)(2,1)S(1)} %pad_maximum_fusion.7), channel_id=1, source_target_pairs={{0,1},{1,2},{2,3},{3,0},{4,5},{5,6},{6,7},{7,4},{8,9},{9,10},{10,1... | collective-permute-start | bytes 1179656 | tf_op jit(solution)/shard_map/ppermute | solution.py:199
  105.4 56.1 %collective-permute-start.1 = (bf16[512,384]{1,0:T(8,128)(2,1)S(1)}, bf16[512,384]{1,0:T(8,128)(2,1)S(1)}, u32[]{:S(2)}, u32[]{:S(2)}) collective-permute-start(bf16[512,384]{1,0:T(8,128)(2,1)S(1)} %pad_maximum_fusion.8), channel_id=1, source_target_pairs={{0,2},{1,3},{2,0},{3,1},{4,6},{5,7},{6,4},{7,5},{8,10},{9,11},{10,... | collective-permute-start | bytes 1179656 | tf_op jit(solution)/shard_map/ppermute | solution.py:199
  111.5 16.9 %copy-start.31 = (bf16[512,384]{1,0:T(8,128)(2,1)}, bf16[512,384]{1,0:T(8,128)(2,1)S(1)}, u32[]{:S(2)}) copy-start(bf16[512,384]{1,0:T(8,128)(2,1)S(1)} %collective-permute-done.6) | copy-start | bytes 1179652
  111.5 49.9 %collective-permute-start.2 = (bf16[512,384]{1,0:T(8,128)(2,1)S(1)}, bf16[512,384]{1,0:T(8,128)(2,1)S(1)}, u32[]{:S(2)}, u32[]{:S(2)}) collective-permute-start(bf16[512,384]{1,0:T(8,128)(2,1)S(1)} %pad_maximum_fusion.9), channel_id=1, source_target_pairs={{0,3},{1,0},{2,1},{3,2},{4,7},{5,4},{6,5},{7,6},{8,11},{9,8},{10,9... | collective-permute-start | bytes 1179656 | tf_op jit(solution)/shard_map/ppermute | solution.py:199
  130.7 30.7 %copy-start.20 = (bf16[512,128]{1,0:T(8,128)(2,1)S(1)}, bf16[512,128]{1,0:T(8,128)(2,1)}, u32[]{:S(2)}) copy-start(bf16[512,128]{1,0:T(8,128)(2,1)} %get-tuple-element.90) | copy-start | bytes 393220
  130.7 30.7 %copy-start.21 = (bf16[512,128]{1,0:T(8,128)(2,1)S(1)}, bf16[512,128]{1,0:T(8,128)(2,1)}, u32[]{:S(2)}) copy-start(bf16[512,128]{1,0:T(8,128)(2,1)} %get-tuple-element.167) | copy-start | bytes 393220
  152.3 9.3 %copy-start = (f32[2048,128]{1,0:T(8,128)}, f32[2048,128]{1,0:T(8,128)S(1)}, u32[]{:S(2)}) copy-start(f32[2048,128]{1,0:T(8,128)S(1)} %get-tuple-element.23.o_ref) | copy-start | bytes 3145732
  183.2 32.6 %copy-start.2 = (f32[2048,128]{1,0:T(8,128)}, f32[2048,128]{1,0:T(8,128)S(1)}, u32[]{:S(2)}) copy-start(f32[2048,128]{1,0:T(8,128)S(1)} %get-tuple-element.22.o_ref) | copy-start | bytes 3145732
  183.3 32.5 %collective-permute-start.5 = (bf16[512,128]{1,0:T(8,128)(2,1)S(1)}, bf16[512,128]{1,0:T(8,128)(2,1)S(1)}, u32[]{:S(2)}, u32[]{:S(2)}) collective-permute-start(bf16[512,128]{1,0:T(8,128)(2,1)S(1)} %get-tuple-element.120), channel_id=1, source_target_pairs={{0,1},{1,2},{2,3},{3,0},{4,5},{5,6},{6,7},{7,4},{8,9},{9,10},{10,1... | collective-permute-start | bytes 393224 | tf_op jit(solution)/shard_map/ppermute | solution.py:213
  200.0 15.8 %collective-permute-start.4 = (bf16[512,128]{1,0:T(8,128)(2,1)S(1)}, bf16[512,128]{1,0:T(8,128)(2,1)S(1)}, u32[]{:S(2)}, u32[]{:S(2)}) collective-permute-start(bf16[512,128]{1,0:T(8,128)(2,1)S(1)} %get-tuple-element.122), channel_id=1, source_target_pairs={{0,2},{1,3},{2,0},{3,1},{4,6},{5,7},{6,4},{7,5},{8,10},{9,11},{10,... | collective-permute-start | bytes 393224 | tf_op jit(solution)/shard_map/ppermute | solution.py:213
  202.3 7.2 %collective-permute-start.3 = (bf16[512,128]{1,0:T(8,128)(2,1)S(1)}, bf16[512,128]{1,0:T(8,128)(2,1)S(1)}, u32[]{:S(2)}, u32[]{:S(2)}) collective-permute-start(bf16[512,128]{1,0:T(8,128)(2,1)S(1)} %get-tuple-element.123), channel_id=1, source_target_pairs={{0,3},{1,0},{2,1},{3,2},{4,7},{5,4},{6,5},{7,6},{8,11},{9,8},{10,9... | collective-permute-start | bytes 393224 | tf_op jit(solution)/shard_map/ppermute | solution.py:213
  202.5 21.7 %collective-permute-start.11 = (bf16[512,128]{1,0:T(8,128)(2,1)S(1)}, bf16[512,128]{1,0:T(8,128)(2,1)S(1)}, u32[]{:S(2)}, u32[]{:S(2)}) collective-permute-start(bf16[512,128]{1,0:T(8,128)(2,1)S(1)} %get-tuple-element.116), channel_id=1, source_target_pairs={{0,1},{1,2},{2,3},{3,0},{4,5},{5,6},{6,7},{7,4},{8,9},{9,10},{10,1... | collective-permute-start | bytes 393224 | tf_op jit(solution)/shard_map/ppermute | solution.py:213
  204.5 19.7 %collective-permute-start.10 = (bf16[512,128]{1,0:T(8,128)(2,1)S(1)}, bf16[512,128]{1,0:T(8,128)(2,1)S(1)}, u32[]{:S(2)}, u32[]{:S(2)}) collective-permute-start(bf16[512,128]{1,0:T(8,128)(2,1)S(1)} %get-tuple-element.118), channel_id=1, source_target_pairs={{0,2},{1,3},{2,0},{3,1},{4,6},{5,7},{6,4},{7,5},{8,10},{9,11},{10,... | collective-permute-start | bytes 393224 | tf_op jit(solution)/shard_map/ppermute | solution.py:213
  209.5 14.6 %collective-permute-start.9 = (bf16[512,128]{1,0:T(8,128)(2,1)S(1)}, bf16[512,128]{1,0:T(8,128)(2,1)S(1)}, u32[]{:S(2)}, u32[]{:S(2)}) collective-permute-start(bf16[512,128]{1,0:T(8,128)(2,1)S(1)} %get-tuple-element.119), channel_id=1, source_target_pairs={{0,3},{1,0},{2,1},{3,2},{4,7},{5,4},{6,5},{7,6},{8,11},{9,8},{10,9... | collective-permute-start | bytes 393224 | tf_op jit(solution)/shard_map/ppermute | solution.py:213
  247.5 13.8 %copy-start.18 = (bf16[1,512,1024]{2,1,0:T(8,128)(2,1)S(1)}, bf16[1,512,1024]{2,1,0:T(8,128)(2,1)}, u32[]{:S(2)}) copy-start(bf16[1,512,1024]{2,1,0:T(8,128)(2,1)} %param.15) | copy-start | bytes 3145732
  274.1 179.8 %reduce-scatter.9.cloned.1.call-start = ((), (), s32[]{:S(2)}) async-start(), calls=%async_computation.9 | async-start | bytes 2359296 | tf_op jit(solution)/shard_map/reduce_scatter | solution.py:327
  274.3 13.2 %copy-start.12 = (f32[512,1024]{1,0:T(8,128)S(1)}, f32[512,1024]{1,0:T(8,128)}, u32[]{:S(2)}) copy-start(f32[512,1024]{1,0:T(8,128)} %copy-done.11) | copy-start | bytes 6291460
  295.5 166.0 %reduce-scatter.7.cloned.1.call-start = ((), (), s32[]{:S(2)}) async-start(), calls=%async_computation.8 | async-start | bytes 12091392 | tf_op jit(solution)/shard_map/reduce_scatter | solution.py:319
  307.9 250.7 %all-reduce.6.cloned.1.call-start = ((), (), s32[]{:S(2)}) async-start(), calls=%async_computation.13 | async-start | bytes 4554752 | tf_op jit(solution)/shard_map/psum | solution.py:330
  311.5 21.4 %copy-start.3 = (f32[2048,128]{1,0:T(8,128)S(1)}, f32[2048,128]{1,0:T(8,128)}, u32[]{:S(2)}) copy-start(f32[2048,128]{1,0:T(8,128)} %copy-done.2) | copy-start | bytes 3145732
  311.8 7.2 %collective-permute-start.14 = (bf16[512,128]{1,0:T(8,128)(2,1)S(1)}, bf16[512,128]{1,0:T(8,128)(2,1)S(1)}, u32[]{:S(2)}, u32[]{:S(2)}) collective-permute-start(bf16[512,128]{1,0:T(8,128)(2,1)S(1)} %get-tuple-element.64), channel_id=1, source_target_pairs={{0,3},{1,0},{2,1},{3,2},{4,7},{5,4},{6,5},{7,6},{8,11},{9,8},{10,9... | collective-permute-start | bytes 393224 | tf_op jit(solution)/shard_map/ppermute | solution.py:199
  313.2 19.6 %collective-permute-start.13 = (bf16[512,128]{1,0:T(8,128)(2,1)S(1)}, bf16[512,128]{1,0:T(8,128)(2,1)S(1)}, u32[]{:S(2)}, u32[]{:S(2)}) collective-permute-start(bf16[512,128]{1,0:T(8,128)(2,1)S(1)} %get-tuple-element.65), channel_id=1, source_target_pairs={{0,2},{1,3},{2,0},{3,1},{4,6},{5,7},{6,4},{7,5},{8,10},{9,11},{10,... | collective-permute-start | bytes 393224 | tf_op jit(solution)/shard_map/ppermute | solution.py:199
  314.4 18.4 %collective-permute-start.12 = (bf16[512,128]{1,0:T(8,128)(2,1)S(1)}, bf16[512,128]{1,0:T(8,128)(2,1)S(1)}, u32[]{:S(2)}, u32[]{:S(2)}) collective-permute-start(bf16[512,128]{1,0:T(8,128)(2,1)S(1)} %get-tuple-element.66), channel_id=1, source_target_pairs={{0,1},{1,2},{2,3},{3,0},{4,5},{5,6},{6,7},{7,4},{8,9},{9,10},{10,1... | collective-permute-start | bytes 393224 | tf_op jit(solution)/shard_map/ppermute | solution.py:199
  314.4 42.1 %collective-permute-start.20 = (bf16[512,128]{1,0:T(8,128)(2,1)S(1)}, bf16[512,128]{1,0:T(8,128)(2,1)S(1)}, u32[]{:S(2)}, u32[]{:S(2)}) collective-permute-start(bf16[512,128]{1,0:T(8,128)(2,1)S(1)} %get-tuple-element.61), channel_id=1, source_target_pairs={{0,3},{1,0},{2,1},{3,2},{4,7},{5,4},{6,5},{7,6},{8,11},{9,8},{10,9... | collective-permute-start | bytes 393224 | tf_op jit(solution)/shard_map/ppermute | solution.py:199
  318.2 40.3 %collective-permute-start.19 = (bf16[512,128]{1,0:T(8,128)(2,1)S(1)}, bf16[512,128]{1,0:T(8,128)(2,1)S(1)}, u32[]{:S(2)}, u32[]{:S(2)}) collective-permute-start(bf16[512,128]{1,0:T(8,128)(2,1)S(1)} %get-tuple-element.62), channel_id=1, source_target_pairs={{0,2},{1,3},{2,0},{3,1},{4,6},{5,7},{6,4},{7,5},{8,10},{9,11},{10,... | collective-permute-start | bytes 393224 | tf_op jit(solution)/shard_map/ppermute | solution.py:199
  319.0 39.5 %collective-permute-start.18 = (bf16[512,128]{1,0:T(8,128)(2,1)S(1)}, bf16[512,128]{1,0:T(8,128)(2,1)S(1)}, u32[]{:S(2)}, u32[]{:S(2)}) collective-permute-start(bf16[512,128]{1,0:T(8,128)(2,1)S(1)} %get-tuple-element.63), channel_id=1, source_target_pairs={{0,1},{1,2},{2,3},{3,0},{4,5},{5,6},{6,7},{7,4},{8,9},{9,10},{10,1... | collective-permute-start | bytes 393224 | tf_op jit(solution)/shard_map/ppermute | solution.py:199
  356.1 28.8 %collective-permute-start.15 = (bf16[512,384]{1,0:T(8,128)(2,1)S(1)}, bf16[512,384]{1,0:T(8,128)(2,1)S(1)}, u32[]{:S(2)}, u32[]{:S(2)}) collective-permute-start(bf16[512,384]{1,0:T(8,128)(2,1)S(1)} %pad_maximum_fusion.13), channel_id=1, source_target_pairs={{0,3},{1,0},{2,1},{3,2},{4,7},{5,4},{6,5},{7,6},{8,11},{9,8},{10,9... | collective-permute-start | bytes 1179656 | tf_op jit(solution)/shard_map/ppermute | solution.py:213
  356.2 38.1 %collective-permute-start.16 = (bf16[512,384]{1,0:T(8,128)(2,1)S(1)}, bf16[512,384]{1,0:T(8,128)(2,1)S(1)}, u32[]{:S(2)}, u32[]{:S(2)}) collective-permute-start(bf16[512,384]{1,0:T(8,128)(2,1)S(1)} %pad_maximum_fusion.14), channel_id=1, source_target_pairs={{0,2},{1,3},{2,0},{3,1},{4,6},{5,7},{6,4},{7,5},{8,10},{9,11},{10,... | collective-permute-start | bytes 1179656 | tf_op jit(solution)/shard_map/ppermute | solution.py:213
  356.5 38.0 %collective-permute-start.17 = (bf16[512,384]{1,0:T(8,128)(2,1)S(1)}, bf16[512,384]{1,0:T(8,128)(2,1)S(1)}, u32[]{:S(2)}, u32[]{:S(2)}) collective-permute-start(bf16[512,384]{1,0:T(8,128)(2,1)S(1)} %pad_maximum_fusion.15), channel_id=1, source_target_pairs={{0,1},{1,2},{2,3},{3,0},{4,5},{5,6},{6,7},{7,4},{8,9},{9,10},{10,1... | collective-permute-start | bytes 1179656 | tf_op jit(solution)/shard_map/ppermute | solution.py:213
  381.9 19.5 %collective-permute-start.21 = (bf16[512,384]{1,0:T(8,128)(2,1)S(1)}, bf16[512,384]{1,0:T(8,128)(2,1)S(1)}, u32[]{:S(2)}, u32[]{:S(2)}) collective-permute-start(bf16[512,384]{1,0:T(8,128)(2,1)S(1)} %pad_maximum_fusion.16), channel_id=1, source_target_pairs={{0,3},{1,0},{2,1},{3,2},{4,7},{5,4},{6,5},{7,6},{8,11},{9,8},{10,9... | collective-permute-start | bytes 1179656 | tf_op jit(solution)/shard_map/ppermute | solution.py:213
  384.3 40.3 %collective-permute-start.22 = (bf16[512,384]{1,0:T(8,128)(2,1)S(1)}, bf16[512,384]{1,0:T(8,128)(2,1)S(1)}, u32[]{:S(2)}, u32[]{:S(2)}) collective-permute-start(bf16[512,384]{1,0:T(8,128)(2,1)S(1)} %pad_maximum_fusion.17), channel_id=1, source_target_pairs={{0,2},{1,3},{2,0},{3,1},{4,6},{5,7},{6,4},{7,5},{8,10},{9,11},{10,... | collective-permute-start | bytes 1179656 | tf_op jit(solution)/shard_map/ppermute | solution.py:213
  384.9 39.7 %collective-permute-start.23 = (bf16[512,384]{1,0:T(8,128)(2,1)S(1)}, bf16[512,384]{1,0:T(8,128)(2,1)S(1)}, u32[]{:S(2)}, u32[]{:S(2)}) collective-permute-start(bf16[512,384]{1,0:T(8,128)(2,1)S(1)} %pad_maximum_fusion.18), channel_id=1, source_target_pairs={{0,1},{1,2},{2,3},{3,0},{4,5},{5,6},{6,7},{7,4},{8,9},{9,10},{10,1... | collective-permute-start | bytes 1179656 | tf_op jit(solution)/shard_map/ppermute | solution.py:213
  395.1 29.8 %copy-start.29 = (bf16[512,1024]{1,0:T(8,128)(2,1)}, bf16[512,1024]{1,0:T(8,128)(2,1)S(1)}, u32[]{:S(2)}) copy-start(bf16[512,1024]{1,0:T(8,128)(2,1)S(1)} %get-tuple-element.133) | copy-start | bytes 3145732
  451.5 10.1 %copy-start.5 = (f32[512,1024]{1,0:T(8,128)S(1)}, f32[512,1024]{1,0:T(8,128)}, u32[]{:S(2)}) copy-start(f32[512,1024]{1,0:T(8,128)} %copy-done.4) | copy-start | bytes 6291460
  461.5 161.9 %reduce-scatter.11.cloned.1.call-start = ((), (), s32[]{:S(2)}) async-start(), calls=%async_computation.10 | async-start | bytes 7077888 | tf_op jit(solution)/shard_map/reduce_scatter | solution.py:362
  558.6 110.7 %all-reduce.4.cloned.1.call-start = ((), (), s32[]{:S(2)}) async-start(), calls=%async_computation.11 | async-start | bytes 1572864 | tf_op jit(solution)/shard_map/psum | solution.py:363
  567.8 56.2 %copy-start.16 = (f32[512,1024]{1,0:T(8,128)S(1)}, f32[512,1024]{1,0:T(8,128)}, u32[]{:S(2)}) copy-start(f32[512,1024]{1,0:T(8,128)} %copy-done.15) | copy-start | bytes 6291460
  (26 other events, 67.1 us)
Sparse Core Ops, SparseCore 0:
  9.9 48.2 all-gather.4
  60.0 27.8 all-gather.6
  89.9 64.3 all-gather.8
  156.0 42.6 all-gather.10
  274.2 56.1 reduce-scatter.12
  333.9 41.2 reduce-scatter.8
  378.7 82.7 reduce-scatter.6
  464.8 93.7 all-reduce.5
  562.0 61.4 reduce-scatter.10
  625.8 43.4 all-reduce.3
